TPU v7x, 256 devices: a whole 4x4x8 slice. The times are simulated.
256 devices in a mesh: ctx: 8 (over z), head: 4 (over x_hi, core), row: 8 (over x_lo, y).
Axes of the slice: x: 4 (x_hi: 2, x_lo: 2; x = x_hi * 2 + x_lo), y: 4, z: 8, core: 2. Of those that a mesh axis runs over, the one named last changes fastest.
Arguments:
- hidden: bfloat16 [3072, 8192], P(('ctx', 'row')), may hold values from -6 to 6
- norm_gain: bfloat16 [8192], replicated, may hold values from 0.099609375 to 1.8984375
- q_weight: bfloat16 [8192, 4096], P(None, ('head', 'row')), may hold values from -0.09375 to 0.09375
- q_bias: bfloat16 [4096], P(('head', 'row')), may hold values from -3 to 3
- key_weight: bfloat16 [8192, 512], P(None, 'head'), may hold values from -0.0625 to 0.0625
- key_bias: bfloat16 [512], P('head'), may hold values from -3 to 3
- value_weight: bfloat16 [8192, 512], P(None, 'head'), may hold values from -0.0625 to 0.0625
- value_bias: bfloat16 [512], P('head'), may hold values from -3 to 3
- o_weight: bfloat16 [4096, 8192], P(('head', 'row')), may hold values from -6 to 6
- cached_key_rows: bfloat16 [32768, 512], P('ctx', 'head'), may hold values from -256 to 256
- cached_value_rows: bfloat16 [32768, 512], P('ctx', 'head'), may hold values from -6 to 6
- keep_blocks: int32 [8, 8], P('ctx'), may hold values from 0 to 31, as said below
- kept_counts: int32 [8], replicated, may hold values from 2 to 8, as said below
- span_start: int32 [1], replicated, may hold values from 32768 to 36863
Outputs:
- output: bfloat16 [3072, 8192], P('ctx', ('head', 'row'))
Inputs may be any that keep to these rules, and one draw needn't show every extreme that they name: `keep_blocks`: row g lists in increasing order the kept_counts[g] distinct kept blocks among group g's 32 prefix blocks; its remaining entries are 0. `kept_counts`: one group keeps 8 blocks and another keeps 8 // 4.
All inputs are finite; a program needn't handle non-finite values.
Results may differ from a plain program's by a relative error of at most 0.014.
Values may be sent and summed in bfloat16 or wider, within the bound.
A program may use at most 128 MiB of HBM per device.

v0:
```python
import math

import jax
import jax.numpy as jnp
from jax import lax
from jax.sharding import PartitionSpec as P

BLOCK = 128


def shifted(shard, axis, by):
    peers = lax.axis_size(axis)
    return lax.ppermute(shard, axis, [(i, (i + by) % peers) for i in range(peers)])


def apply_rotary(values, token_positions):
    middle = values.shape[-1] // 2
    steps_range = jnp.arange(middle, dtype=jnp.float32)
    frequency = 1000000.0 ** (-2.0 * steps_range / values.shape[-1])
    angles = token_positions.astype(jnp.float32)[:, None] * frequency[None, :]
    cosine = jnp.cos(angles)[:, None, :]
    sine_part = jnp.sin(angles)[:, None, :]
    first_half = values[..., :middle]
    second_half = values[..., middle:]
    return jnp.concatenate(
        [
            first_half * cosine - second_half * sine_part,
            second_half * cosine + first_half * sine_part,
        ],
        axis=-1,
    )


def local(
    hidden,
    norm_gain,
    q_weight,
    q_bias,
    key_weight,
    key_bias,
    value_weight,
    value_bias,
    o_weight,
    cached_key_rows,
    cached_value_rows,
    keep_blocks,
    kept_counts,
    span_start,
):
    cycle_size = lax.axis_size("ctx")
    group_index = lax.axis_index("ctx")
    row_count = lax.axis_size("row")
    own_rows = hidden.shape[0]
    group_rows = own_rows * row_count
    head_size = key_weight.shape[1]
    query_heads = q_weight.shape[1] // head_size
    query_width = query_heads * head_size
    widened = hidden.astype(jnp.float32)
    rms_factor = lax.rsqrt(jnp.mean(widened * widened, axis=-1, keepdims=True) + 1e-06)
    normed = (widened * rms_factor * norm_gain.astype(jnp.float32)).astype(jnp.bfloat16)
    first_token = span_start[0] + group_index * group_rows
    query_shift = q_bias.astype(jnp.float32)
    key_shift = key_bias.astype(jnp.float32)
    value_shift = value_bias.astype(jnp.float32)
    piece = lax.all_gather(normed, "row", axis=0, tiled=True)
    projected = jnp.dot(piece, q_weight, preferred_element_type=jnp.float32) + query_shift
    key_part = jnp.dot(piece, key_weight, preferred_element_type=jnp.float32) + key_shift
    value_part = jnp.dot(piece, value_weight, preferred_element_type=jnp.float32) + value_shift
    projected = jnp.concatenate([projected, key_part, value_part], axis=1)
    token_positions = first_token + jnp.arange(group_rows, dtype=jnp.int32)
    queries = apply_rotary(
        projected[:, :query_width].reshape(group_rows, query_heads, head_size), token_positions
    ).astype(jnp.bfloat16)
    key_rows = projected[:, query_width : query_width + head_size].reshape(group_rows, 1, head_size)
    span_keys = (
        apply_rotary(key_rows, token_positions).reshape(group_rows, head_size).astype(jnp.bfloat16)
    )
    span_values = projected[:, query_width + head_size :].astype(jnp.bfloat16)
    span_pair = jnp.stack([span_keys, span_values])
    kept_here = keep_blocks[0]
    row_numbers = (
        kept_here[:, None] * BLOCK + jnp.arange(BLOCK, dtype=jnp.int32)[None, :]
    ).reshape(-1)
    prefix_pair = jnp.stack(
        [
            jnp.take(cached_key_rows, row_numbers, axis=0),
            jnp.take(cached_value_rows, row_numbers, axis=0),
        ]
    )
    buffer = jnp.concatenate([prefix_pair, span_pair], axis=1)
    prefix_slots = prefix_pair.shape[1]
    score_scale = 1.0 / math.sqrt(head_size)
    key_position = jnp.arange(buffer.shape[1], dtype=jnp.int32)
    query_token = group_index * group_rows + jnp.arange(group_rows, dtype=jnp.int32)

    def attend_block(carried, travelling, source):
        row_max, denominator, blended = carried
        scores = (
            jnp.einsum("tqd,sd->tqs", queries, travelling[0], preferred_element_type=jnp.float32)
            * score_scale
        )
        live_prefix = key_position // BLOCK < kept_counts[source]
        span_token = source * group_rows + key_position - prefix_slots
        visible = jnp.where(
            key_position[None, :] < prefix_slots,
            live_prefix[None, :],
            span_token[None, :] <= query_token[:, None],
        )
        scores = jnp.where(visible[:, None, :], scores, -jnp.inf)
        new_max = jnp.maximum(row_max, scores.max(axis=-1))
        shrink = jnp.exp(row_max - new_max)
        weights = jnp.exp(scores - new_max[..., None])
        denominator = denominator * shrink + weights.sum(axis=-1)
        blended = blended * shrink[..., None] + jnp.einsum(
            "tqs,sd->tqd",
            weights.astype(jnp.bfloat16),
            travelling[1],
            preferred_element_type=jnp.float32,
        )
        return (new_max, denominator, blended)

    carried = (
        jnp.full((group_rows, query_heads), -jnp.inf, jnp.float32),
        jnp.zeros((group_rows, query_heads), jnp.float32),
        jnp.zeros((group_rows, query_heads, head_size), jnp.float32),
    )
    carried = attend_block(carried, buffer, group_index)

    def forward_step(step_number, loop_state):
        state_now, travelling = loop_state
        travelling = shifted(travelling, "ctx", 1)
        source = (group_index - step_number - 1) % cycle_size
        return (attend_block(state_now, travelling, source), travelling)

    carried, buffer = lax.fori_loop(0, cycle_size - 1, forward_step, (carried, buffer))
    row_max, denominator, blended = carried
    attended = (
        (blended / denominator[..., None]).astype(jnp.bfloat16).reshape(group_rows, query_width)
    )
    summed = lax.psum_scatter(
        lax.dot_general(
            o_weight, attended, (((0,), (1,)), ((), ())), preferred_element_type=jnp.float32
        ),
        ("head", "row"),
        scatter_dimension=0,
        tiled=True,
    )
    result = summed.T.astype(jnp.bfloat16)
    return result


def solution(mesh):
    in_specs = (
        P(("ctx", "row"), None),
        P(),
        P(None, ("head", "row")),
        P(("head", "row")),
        P(None, "head"),
        P("head"),
        P(None, "head"),
        P("head"),
        P(("head", "row"), None),
        P("ctx", "head"),
        P("ctx", "head"),
        P("ctx", None),
        P(),
        P(),
    )
    out_specs = P("ctx", ("head", "row"))
    return jax.shard_map(local, mesh=mesh, in_specs=in_specs, out_specs=out_specs, check_vma=False)
```

profile of v0, /device:TPU:1, one launch (start us, length us, event | category | flops | bytes accessed | tf_op | source)
XLA Modules:
  0.0 415.7 jit_solution(7106769122406162033)
XLA Ops:
  6.6 1.5 fusion.23
  8.9 2.3 fusion.25
  12.1 3.2 gather_fusion.1
  15.3 4.2 %gather_fusion = bf16[1024,128]{1,0:T(8,128)(2,1)S(1)} fusion(bf16[4096,128]{1,0:T(8,128)(2,1)} %param.27, s32[1024]{0:T(1024)S(1)} %fusion.57), kind=kCustom, calls=%fused_computation.clone | custom fusion | bytes 528384 | tf_op jit(solution)/shard_map/jit(_take)/gather | solution.py:86
  21.0 69.0 %all-gather.2.cloned.1.call-done = bf16[384,8192]{1,0:T(8,128)(2,1)} async-done(((bf16[48,8192]{1,0:T(8,128)(2,1)}), bf16[384,8192]{1,0:T(8,128)(2,1)}) %all-gather.2.cloned.1.call-update) | async-done | bytes 6291472 | tf_op jit(solution)/shard_map/all_gather | solution.py:65
  90.0 5.4 %fusion.27 = f32[384,1,128]{0,2,1:T(8,128)S(1)} fusion(bf16[384,8192]{1,0:T(8,128)(2,1)} %all-gather.2.cloned.1.call-done, bf16[8192,128]{1,0:T(8,128)(2,1)} %param.22, f32[128]{0:T(128)S(1)} %convert_element_type.80), kind=kOutput, calls=%fused_computation.47 | convolution fusion | flops 805355520 | bytes 8585728 | tf_op jit(solution)/shard_map/dot_general | solution.py:67
  95.8 1.9 fusion.28
  98.3 2.0 fusion.30
  100.4 0.9 pad_maximum_fusion
  101.4 3.1 fusion.63
  104.6 2.2 fusion.22
  106.8 1.5 fusion.26
  108.3 131.5 %while.24 = (s32[]{:T(128)}, f32[384,1]{0,1:T(1,128)S(1)}, f32[384,1]{0,1:T(1,128)S(1)}, f32[384,1,128]{2,0,1:T(8,128)S(1)}, bf16[2,1408,128]{2,1,0:T(8,128)(2,1...) while((s32[]{:T(128)}, f32[384,1]{0,1:T(1,128)S(1)}, ...), condition=%wide.region_6.8_spmd.clone.clone, body=%wide.region_3.7_spmd.clone.clone.sunk | while | flops 281806848 | bytes 12080512 | solution.py:135
  108.3 1.4 collective-permute-start
  111.1 16.4 %collective-permute-done = bf16[2,1408,128]{2,1,0:T(8,128)(2,1)S(1)} collective-permute-done((bf16[2,1408,128]{2,1,0:T(8,128)(2,1)}, bf16[2,1408,128]{2,1,0:T(8,128)(2,1)S(1)}, u32[]{:S(2)}, u32[]{:S(2)}) %collective-permute-start) | collective-permute-done | bytes 720928 | tf_op jit(solution)/shard_map/while/body/eval_jaxpr/ppermute | solution.py:13
  131.7 16.4 %collective-permute-done = bf16[2,1408,128]{2,1,0:T(8,128)(2,1)S(1)} collective-permute-done((bf16[2,1408,128]{2,1,0:T(8,128)(2,1)}, bf16[2,1408,128]{2,1,0:T(8,128)(2,1)S(1)}, u32[]{:S(2)}, u32[]{:S(2)}) %collective-permute-start) | collective-permute-done | bytes 720928 | tf_op jit(solution)/shard_map/while/body/eval_jaxpr/ppermute | solution.py:13
  152.3 15.4 %collective-permute-done = bf16[2,1408,128]{2,1,0:T(8,128)(2,1)S(1)} collective-permute-done((bf16[2,1408,128]{2,1,0:T(8,128)(2,1)}, bf16[2,1408,128]{2,1,0:T(8,128)(2,1)S(1)}, u32[]{:S(2)}, u32[]{:S(2)}) %collective-permute-start) | collective-permute-done | bytes 720928 | tf_op jit(solution)/shard_map/while/body/eval_jaxpr/ppermute | solution.py:13
  172.0 14.5 %collective-permute-done = bf16[2,1408,128]{2,1,0:T(8,128)(2,1)S(1)} collective-permute-done((bf16[2,1408,128]{2,1,0:T(8,128)(2,1)}, bf16[2,1408,128]{2,1,0:T(8,128)(2,1)S(1)}, u32[]{:S(2)}, u32[]{:S(2)}) %collective-permute-start) | collective-permute-done | bytes 720928 | tf_op jit(solution)/shard_map/while/body/eval_jaxpr/ppermute | solution.py:13
  190.7 13.6 %collective-permute-done = bf16[2,1408,128]{2,1,0:T(8,128)(2,1)S(1)} collective-permute-done((bf16[2,1408,128]{2,1,0:T(8,128)(2,1)}, bf16[2,1408,128]{2,1,0:T(8,128)(2,1)S(1)}, u32[]{:S(2)}, u32[]{:S(2)}) %collective-permute-start) | collective-permute-done | bytes 720928 | tf_op jit(solution)/shard_map/while/body/eval_jaxpr/ppermute | solution.py:13
  208.5 12.7 %collective-permute-done = bf16[2,1408,128]{2,1,0:T(8,128)(2,1)S(1)} collective-permute-done((bf16[2,1408,128]{2,1,0:T(8,128)(2,1)}, bf16[2,1408,128]{2,1,0:T(8,128)(2,1)S(1)}, u32[]{:S(2)}, u32[]{:S(2)}) %collective-permute-start) | collective-permute-done | bytes 720928 | tf_op jit(solution)/shard_map/while/body/eval_jaxpr/ppermute | solution.py:13
  225.4 11.8 %collective-permute-done = bf16[2,1408,128]{2,1,0:T(8,128)(2,1)S(1)} collective-permute-done((bf16[2,1408,128]{2,1,0:T(8,128)(2,1)}, bf16[2,1408,128]{2,1,0:T(8,128)(2,1)S(1)}, u32[]{:S(2)}, u32[]{:S(2)}) %collective-permute-start) | collective-permute-done | bytes 720928 | tf_op jit(solution)/shard_map/while/body/eval_jaxpr/ppermute | solution.py:13
  239.9 6.4 %convolution_bitcast_fusion.1 = f32[8192,384]{0,1:T(8,128)} fusion(bf16[128,8192]{1,0:T(8,128)(2,1)S(1)} %copy-done, f32[384,1,128]{2,0,1:T(8,128)S(1)} %get-tuple-element.311, f32[384]{0:T(512)S(1)} %reduce.23), kind=kOutput, calls=%fused_computation.32 | convolution fusion | flops 805404672 | bytes 14878208 | tf_op jit(solution)/shard_map/dot_general | solution.py:141
  246.3 160.8 %reduce-scatter.2.cloned.1.call-done = f32[256,384]{0,1:T(8,128)} async-done(((f32[8192,384]{0,1:T(8,128)}), f32[256,384]{0,1:T(8,128)}) %reduce-scatter.2.cloned.1.call-update) | async-done | bytes 393232 | tf_op jit(solution)/shard_map/reduce_scatter | solution.py:140
  407.1 1.7 convert_bitcast_fusion
  (140 shorter events, 32.6 us)
Async XLA Ops:
  6.5 233.3 %copy-start = (bf16[128,8192]{1,0:T(8,128)(2,1)S(1)}, bf16[128,8192]{1,0:T(8,128)(2,1)}, u32[]{:S(2)}) copy-start(bf16[128,8192]{1,0:T(8,128)(2,1)} %param.26) | copy-start | bytes 6291460
  6.5 5.4 %copy-start.6 = (bf16[128]{0:T(256)(128)(2,1)S(1)}, bf16[128]{0:T(256)(128)(2,1)}, u32[]{:S(2)}) copy-start(bf16[128]{0:T(256)(128)(2,1)} %param.21) | copy-start | bytes 772
  6.5 5.4 %copy-start.7 = (bf16[128]{0:T(256)(128)(2,1)S(1)}, bf16[128]{0:T(256)(128)(2,1)}, u32[]{:S(2)}) copy-start(bf16[128]{0:T(256)(128)(2,1)} %param.23) | copy-start | bytes 772
  6.5 5.4 %copy-start.8 = (bf16[128]{0:T(256)(128)(2,1)S(1)}, bf16[128]{0:T(256)(128)(2,1)}, u32[]{:S(2)}) copy-start(bf16[128]{0:T(256)(128)(2,1)} %param.25) | copy-start | bytes 772
  6.5 5.4 %copy-start.9 = (s32[1,8]{1,0:T(1,128)S(1)}, s32[1,8]{1,0:T(1,128)}, u32[]{:S(2)}) copy-start(s32[1,8]{1,0:T(1,128)} %param.29) | copy-start | bytes 100
  6.5 5.5 %copy-start.3 = (bf16[4096,128]{1,0:T(8,128)(2,1)S(1)}, bf16[4096,128]{1,0:T(8,128)(2,1)}, u32[]{:S(2)}) copy-start(bf16[4096,128]{1,0:T(8,128)(2,1)} %param.28) | copy-start | bytes 3145732
  6.6 83.4 %all-gather.2.cloned.1.call-start = ((), (), s32[]{:S(2)}) async-start(), calls=%async_computation.1 | async-start | bytes 7077888 | tf_op jit(solution)/shard_map/all_gather | solution.py:65
  11.2 395.9 %reduce-scatter.2.cloned.1.call-start = ((), (), s32[]{:S(2)}) async-start(), calls=%async_computation.2 | async-start | bytes 12976128 | tf_op jit(solution)/shard_map/reduce_scatter | solution.py:140
  12.0 7.5 %copy-start.10 = (s32[8]{0:T(128)S(1)}, s32[8]{0:T(128)}, u32[]{:S(2)}) copy-start(s32[8]{0:T(128)} %param.30) | copy-start | bytes 100
  90.0 5.5 %copy-start.1 = (bf16[384,8192]{1,0:T(8,128)(2,1)S(1)}, bf16[384,8192]{1,0:T(8,128)(2,1)}, u32[]{:S(2)}) copy-start(bf16[384,8192]{1,0:T(8,128)(2,1)} %all-gather.2.cloned.1.call-done) | copy-start | bytes 18874372
  90.0 5.8 %copy-start.4 = (bf16[8192,128]{1,0:T(8,128)(2,1)S(1)}, bf16[8192,128]{1,0:T(8,128)(2,1)}, u32[]{:S(2)}) copy-start(bf16[8192,128]{1,0:T(8,128)(2,1)} %param.20) | copy-start | bytes 6291460
  95.8 2.5 copy-start.5
  104.6 2.3 copy-start.2
  108.3 19.2 %collective-permute-start = (bf16[2,1408,128]{2,1,0:T(8,128)(2,1)}, bf16[2,1408,128]{2,1,0:T(8,128)(2,1)S(1)}, u32[]{:S(2)}, u32[]{:S(2)}) collective-permute-start(bf16[2,1408,128]{2,1,0:T(8,128)(2,1)} %get-tuple-element.511), channel_id=1, source_target_pairs={{0,32},{32,64},{64,96},{96,128},{128,160},{160,192},{192,224},{224... | collective-permute-start | bytes 2162696 | tf_op jit(solution)/shard_map/while/body/eval_jaxpr/ppermute | solution.py:13
  130.2 17.9 %collective-permute-start = (bf16[2,1408,128]{2,1,0:T(8,128)(2,1)}, bf16[2,1408,128]{2,1,0:T(8,128)(2,1)S(1)}, u32[]{:S(2)}, u32[]{:S(2)}) collective-permute-start(bf16[2,1408,128]{2,1,0:T(8,128)(2,1)} %get-tuple-element.511), channel_id=1, source_target_pairs={{0,32},{32,64},{64,96},{96,128},{128,160},{160,192},{192,224},{224... | collective-permute-start | bytes 2162696 | tf_op jit(solution)/shard_map/while/body/eval_jaxpr/ppermute | solution.py:13
  150.8 17.0 %collective-permute-start = (bf16[2,1408,128]{2,1,0:T(8,128)(2,1)}, bf16[2,1408,128]{2,1,0:T(8,128)(2,1)S(1)}, u32[]{:S(2)}, u32[]{:S(2)}) collective-permute-start(bf16[2,1408,128]{2,1,0:T(8,128)(2,1)} %get-tuple-element.511), channel_id=1, source_target_pairs={{0,32},{32,64},{64,96},{96,128},{128,160},{160,192},{192,224},{224... | collective-permute-start | bytes 2162696 | tf_op jit(solution)/shard_map/while/body/eval_jaxpr/ppermute | solution.py:13
  170.4 16.1 %collective-permute-start = (bf16[2,1408,128]{2,1,0:T(8,128)(2,1)}, bf16[2,1408,128]{2,1,0:T(8,128)(2,1)S(1)}, u32[]{:S(2)}, u32[]{:S(2)}) collective-permute-start(bf16[2,1408,128]{2,1,0:T(8,128)(2,1)} %get-tuple-element.511), channel_id=1, source_target_pairs={{0,32},{32,64},{64,96},{96,128},{128,160},{160,192},{192,224},{224... | collective-permute-start | bytes 2162696 | tf_op jit(solution)/shard_map/while/body/eval_jaxpr/ppermute | solution.py:13
  189.2 15.1 %collective-permute-start = (bf16[2,1408,128]{2,1,0:T(8,128)(2,1)}, bf16[2,1408,128]{2,1,0:T(8,128)(2,1)S(1)}, u32[]{:S(2)}, u32[]{:S(2)}) collective-permute-start(bf16[2,1408,128]{2,1,0:T(8,128)(2,1)} %get-tuple-element.511), channel_id=1, source_target_pairs={{0,32},{32,64},{64,96},{96,128},{128,160},{160,192},{192,224},{224... | collective-permute-start | bytes 2162696 | tf_op jit(solution)/shard_map/while/body/eval_jaxpr/ppermute | solution.py:13
  207.0 14.2 %collective-permute-start = (bf16[2,1408,128]{2,1,0:T(8,128)(2,1)}, bf16[2,1408,128]{2,1,0:T(8,128)(2,1)S(1)}, u32[]{:S(2)}, u32[]{:S(2)}) collective-permute-start(bf16[2,1408,128]{2,1,0:T(8,128)(2,1)} %get-tuple-element.511), channel_id=1, source_target_pairs={{0,32},{32,64},{64,96},{96,128},{128,160},{160,192},{192,224},{224... | collective-permute-start | bytes 2162696 | tf_op jit(solution)/shard_map/while/body/eval_jaxpr/ppermute | solution.py:13
  223.9 13.3 %collective-permute-start = (bf16[2,1408,128]{2,1,0:T(8,128)(2,1)}, bf16[2,1408,128]{2,1,0:T(8,128)(2,1)S(1)}, u32[]{:S(2)}, u32[]{:S(2)}) collective-permute-start(bf16[2,1408,128]{2,1,0:T(8,128)(2,1)} %get-tuple-element.511), channel_id=1, source_target_pairs={{0,32},{32,64},{64,96},{96,128},{128,160},{160,192},{192,224},{224... | collective-permute-start | bytes 2162696 | tf_op jit(solution)/shard_map/while/body/eval_jaxpr/ppermute | solution.py:13
Sparse Core Ops, SparseCore 0:
  11.3 78.6 all-gather.1
  246.4 160.6 reduce-scatter.1
where the time goes:
time: 423 us; the launch traced here: 416 us
  waiting for transfers between devices  331 us (78%)
  matrix products  29.2 us (7%)
  local copies, waits for them, and re-layouts  19.6 us (5%)
  other arithmetic  19.5 us (5%)
  between operations  14.3 us (3%)
    reduce_scatter x1, waiting for transfers between devices, local(): lax.psum_scatter(lax.dot_general(o_weight, attended, (((0,), (1,)), ((),...  161 us
    ppermute x7, waiting for transfers between devices, shifted(): lax.ppermute(shard, axis, [(i, (i + by) % peers) for i in range(peers)])  101 us
    all_gather x1, waiting for transfers between devices, local(): piece = lax.all_gather(normed, 'row', axis=0, tiled=True)  69 us
  transfers between devices with their start and end apart: 9, of which 9 were waited for; matrix products, arithmetic and copies ran while one was open for 5% of the time, Pallas kernels for 0%

commit v1 on v0

v1 whole, which is shorter than its diff:
```python
import math

import jax
import jax.numpy as jnp
from jax import lax
from jax.experimental import pallas as pl
from jax.experimental.pallas import tpu as pltpu
from jax.sharding import PartitionSpec as P

MESH = pl.DeviceIdType.MESH
F32 = jnp.float32
BF16 = jnp.bfloat16

N_CTX = 8
WIDTH = 8192
HALF = 4096
QUART = 2048
HEAD = 128
BLOCK = 128
KEEP = 8
SHARDS = 8
SHARD = 48
CHUNKS = 3
PIECE = 16
CHUNK = SHARDS * PIECE
GROUP = SHARDS * SHARD
KEPT = KEEP * BLOCK
NEG = -1e30
LOG2E = math.log2(math.e)


def nt_dot(a, b):
    return lax.dot_general(a, b, (((1,), (1,)), ((), ())), preferred_element_type=F32)


def nn_dot(a, b):
    return lax.dot_general(a, b, (((1,), (0,)), ((), ())), preferred_element_type=F32)


def keep_kernel(blocks_ref, counts_ref, k_ref, v_ref, kept_k_ref, kept_v_ref, mask_ref, sems):
    copies = []
    for j in range(KEEP):
        source = pl.ds(pl.multiple_of(blocks_ref[0, j] * BLOCK, BLOCK), BLOCK)
        for i, (whole, kept) in enumerate(((k_ref, kept_k_ref), (v_ref, kept_v_ref))):
            copy = pltpu.make_async_copy(whole.at[source, :], kept.at[pl.ds(j * BLOCK, BLOCK), :], sems.at[i, j])
            copy.start()
            copies.append(copy)
    z = lax.axis_index("ctx")
    for s in range(3):
        live = counts_ref[lax.rem(z + s + 7, 8)]
        slot = lax.broadcasted_iota(jnp.int32, (1, KEPT), 1) // BLOCK
        mask_ref[s] = jnp.where(slot < live, 0.0, NEG).astype(F32)
    for copy in copies:
        copy.wait()


def kernel(
    hidden_ref, gain_ref, qw_ref, qb_ref, kw_ref, kb_ref, vw_ref, vb_ref, ow_ref, kept_k_ref, kept_v_ref,
    mask, cos_ref, sin_ref,
    out_ref,
    normed, gathered, q_mat, kv_mat, o_mat,
    pre_k, pre_v, span_k, span_v,
    halves, halves_in, queries, part_o, part_s, part_o_in, part_s_in,
    own_o, own_m, attended, one_out, one_in, mid, two_out, two_in,
    local_sems, a_send, a_recv, w_send, w_recv, pre_send, pre_recv, row_send, row_recv, span_send, span_recv,
    h_send, h_recv, q_send, q_recv, p_send, p_recv, t_send, t_recv, one_send, one_recv, two_send, two_recv,
):
    z = lax.axis_index("ctx")
    head = lax.axis_index("head")
    row = lax.axis_index("row")
    core = lax.rem(head, 2)
    x_lo = row // 4
    y = lax.rem(row, 4)
    x = 2 * (head // 2) + x_lo
    other = 1 - core

    def device(dz, dx, dy, dc=None):
        xx = lax.rem(x + dx + 4, 4)
        yy = lax.rem(y + dy + 4, 4)
        cc = core if dc is None else dc
        return (lax.rem(z + dz + 8, 8), 2 * (xx // 2) + cc, 4 * lax.rem(xx, 2) + yy)

    def row_peer(step):
        return (z, head, lax.rem(row + step, SHARDS))

    partner = (z, 2 * (head // 2) + other, row)

    def remote(src, dst, send, recv, to):
        return pltpu.make_async_remote_copy(
            src_ref=src, dst_ref=dst, send_sem=send, recv_sem=recv, device_id=to, device_id_type=MESH
        )

    sent = []

    def send(src, dst, send_sem, recv_sem, to):
        copy = remote(src, dst, send_sem, recv_sem, to)
        copy.start()
        sent.append(copy)

    def arrive(dst, recv_sem):
        remote(dst, dst, recv_sem, recv_sem, partner).wait_recv()

    def load(src, dst, i):
        copy = pltpu.make_async_copy(src, dst, local_sems.at[i])
        copy.start()
        return copy

    load_k = load(kept_k_ref, pre_k.at[1], 0)
    load_v = load(kept_v_ref, pre_v.at[1, :, 0:HEAD], 1)
    load_kw = load(kw_ref, kv_mat.at[:, 0:HEAD], 2)
    load_vw = load(vw_ref, kv_mat.at[:, HEAD : 2 * HEAD], 3)
    own_cols = pl.ds(pl.multiple_of(core * HEAD, HEAD), HEAD)
    load_qw = load(qw_ref.at[pl.ds(pl.multiple_of(core * HALF, HALF), HALF), :], q_mat.at[:, own_cols], 4)

    def column(cc, first, second):
        xx = first * (1 - cc) + second * cc
        yy = second * (1 - cc) + first * cc
        return pl.multiple_of((2 * (xx // 2) + cc) * 2048 + (4 * lax.rem(xx, 2) + yy) * 256, 256)

    for b1 in range(4):
        for b2 in range(4):
            pltpu.make_async_copy(
                ow_ref.at[:, pl.ds(column(core, b1, b2), 256)],
                o_mat.at[b1, own_cols, pl.ds(b2 * 256, 256)],
                local_sems.at[5],
            ).start()

    barrier = pltpu.get_barrier_semaphore()
    partners = [partner]
    partners += [device(0, 1, 0), device(0, -1, 0)]
    partners += [row_peer(s) for s in range(1, SHARDS)]
    partners += [device(dz, 0, 0) for dz in (1, -1, 3, -3)]
    for to in partners:
        pl.semaphore_signal(barrier, inc=1, device_id=to, device_id_type=MESH)
    pl.semaphore_wait(barrier, len(partners))

    total = jnp.zeros((SHARD, 1), F32)
    for i in range(8):
        part = hidden_ref[:, i * 1024 : (i + 1) * 1024].astype(F32)
        total = total + jnp.sum(part * part, axis=1, keepdims=True)
    factor = lax.rsqrt(total / WIDTH + 1e-6)
    for i in range(8):
        cols = slice(i * 1024, (i + 1) * 1024)
        part = hidden_ref[:, cols].astype(F32) * factor * gain_ref[:, cols].astype(F32)
        normed[:, cols] = part.astype(BF16)

    def rows_of(shard):
        return pl.ds(pl.multiple_of(shard * PIECE, PIECE), PIECE)

    for k in range(CHUNKS):
        for f in range(2):
            cols = pl.ds(pl.multiple_of(core * HALF + f * QUART, QUART), QUART)
            gathered[k, f, rows_of(row), :] = normed[k * PIECE : (k + 1) * PIECE, cols]

    y_up, y_down = device(0, 0, 1), device(0, 0, -1)
    x_up, x_down = device(0, 1, 0), device(0, -1, 0)
    a_count = [0, 0, 0]

    def forward(k, f, shard, to):
        piece = gathered.at[k, f, rows_of(shard), :]
        send(piece, piece, a_send.at[k, a_count[k]], a_recv.at[k, f, shard], to)
        a_count[k] += 1

    def shard_at(dy, flip=False):
        xl = 1 - x_lo if flip else x_lo
        return 4 * xl + lax.rem(y + dy + 4, 4)

    def a_arrive(k, f, shard):
        arrive(gathered.at[k, f, rows_of(shard), :], a_recv.at[k, f, shard])

    def a_start(k):
        forward(k, 0, row, x_up)
        forward(k, 0, row, y_up)
        forward(k, 1, row, x_down)
        forward(k, 1, row, y_down)
        forward(k, 1, row, y_up)
        forward(k, 0, row, y_down)

    def a_mid(k):
        below, above = shard_at(-1), shard_at(1)
        a_arrive(k, 0, below)
        forward(k, 0, below, y_up)
        forward(k, 0, below, x_up)
        a_arrive(k, 1, above)
        forward(k, 1, above, y_down)
        forward(k, 1, above, x_down)
        a_arrive(k, 1, below)
        forward(k, 1, below, x_down)
        a_arrive(k, 0, above)
        forward(k, 0, above, x_up)

    def a_last(k):
        far = shard_at(2)
        a_arrive(k, 0, far)
        forward(k, 0, far, x_up)
        a_arrive(k, 1, far)
        forward(k, 1, far, x_down)

    for k in range(CHUNKS):
        a_start(k)

    send(
        qw_ref.at[pl.ds(pl.multiple_of(other * HALF, HALF), HALF), :],
        q_mat.at[:, own_cols], w_send.at[0], w_recv.at[0], partner,
    )
    for b1 in range(4):
        for b2 in range(4):
            remote(
                ow_ref.at[:, pl.ds(column(other, b1, b2), 256)],
                o_mat.at[b1, own_cols, pl.ds(b2 * 256, 256)],
                w_send.at[1], w_recv.at[1], partner,
            ).start()

    load_k.wait()
    load_v.wait()
    z_up, z_down = device(1, 0, 0), device(-1, 0, 0)
    left = pl.ds(0, HEAD)
    for i, (slot, to) in enumerate(((0, z_up), (2, z_down))):
        send(pre_k.at[1], pre_k.at[slot], pre_send.at[0, i], pre_recv.at[0, slot], to)
        send(pre_v.at[1, :, left], pre_v.at[slot, :, left], pre_send.at[1, i], pre_recv.at[1, slot], to)

    for s in range(3):
        pre_v[s, :, HEAD : 2 * HEAD] = jnp.ones((KEPT, HEAD), BF16)
        span_v[s, :, HEAD : 2 * HEAD] = jnp.ones((GROUP, HEAD), BF16)

    def rotated(values, cosine, sine):
        return values * cosine + pltpu.roll(values, HEAD // 2, 1) * sine

    load_kw.wait()
    load_vw.wait()

    def kv_step(i, total):
        at = pl.ds(pl.multiple_of(i * 1024, 1024), 1024)
        return total + nn_dot(normed[:, at], kv_mat[at, :])

    pair = lax.fori_loop(0, 8, kv_step, jnp.zeros((SHARD, 2 * HEAD), F32))
    key_part = pair[:, 0:HEAD] + kb_ref[...].astype(F32)
    value_part = pair[:, HEAD : 2 * HEAD] + vb_ref[...].astype(F32)
    own_cos = jnp.concatenate([cos_ref[k, rows_of(row), :] for k in range(CHUNKS)], axis=0)
    own_sin = jnp.concatenate([sin_ref[k, rows_of(row), :] for k in range(CHUNKS)], axis=0)

    def span_rows(shard):
        return pl.ds(pl.multiple_of(shard * SHARD, SHARD), SHARD)

    span_k[1, span_rows(row), :] = rotated(key_part, own_cos, own_sin).astype(BF16)
    span_v[1, span_rows(row), 0:HEAD] = value_part.astype(BF16)
    for s in range(1, SHARDS):
        here = span_k.at[1, span_rows(row), :]
        send(here, here, row_send.at[0, s], row_recv.at[0, row], row_peer(s))
        here = span_v.at[1, span_rows(row), left]
        send(here, here, row_send.at[1, s], row_recv.at[1, row], row_peer(s))

    def span_forward():
        for s in range(1, SHARDS):
            peer = lax.rem(row + s, SHARDS)
            arrive(span_k.at[1, span_rows(peer), :], row_recv.at[0, peer])
            arrive(span_v.at[1, span_rows(peer), left], row_recv.at[1, peer])
        for i, (slot, to) in enumerate(((0, z_up), (2, z_down))):
            send(span_k.at[1], span_k.at[slot], span_send.at[0, i], span_recv.at[0, slot], to)
            send(span_v.at[1, :, left], span_v.at[slot, :, left], span_send.at[1, i], span_recv.at[1, slot], to)

    def neighbours_arrive():
        for slot in (0, 2):
            arrive(pre_k.at[slot], pre_recv.at[0, slot])
            arrive(pre_v.at[slot, :, left], pre_recv.at[1, slot])
            arrive(span_k.at[slot], span_recv.at[0, slot])
            arrive(span_v.at[slot, :, left], span_recv.at[1, slot])

    def project(k):
        for shard_dy in range(4):
            for f in range(2):
                a_arrive(k, f, shard_at(shard_dy, True))
        both = nn_dot(gathered[k, 0], q_mat[0:QUART, :]) + nn_dot(gathered[k, 1], q_mat[QUART:HALF, :])
        halves[k, 0] = both[:, 0:HEAD]
        halves[k, 1] = both[:, HEAD : 2 * HEAD]
        send(halves.at[k, other], halves_in.at[k], h_send.at[k], h_recv.at[k], partner)

    def finish_queries(k):
        arrive(halves_in.at[k], h_recv.at[k])
        values = halves[k, core] + halves_in[k] + qb_ref[...].astype(F32)
        values = rotated(values, cos_ref[k], sin_ref[k]) * (LOG2E / math.sqrt(HEAD))
        queries[0, k] = values.astype(BF16)
        send(queries.at[0, k], queries.at[1, k], q_send.at[k, 0], q_recv.at[k, 0], device(3, 0, 0))
        send(queries.at[0, k], queries.at[2, k], q_send.at[k, 1], q_recv.at[k, 1], device(-3, 0, 0))

    token = lax.broadcasted_iota(jnp.int32, (CHUNK, 1), 0)
    token = (token // PIECE) * SHARD + lax.rem(token, PIECE)
    key_token = lax.broadcasted_iota(jnp.int32, (1, GROUP), 1)

    def attend(k, source, first, last):
        query = queries[source, k]
        query_group = lax.rem(z + (0, 5, 3)[source], 8)
        query_token = query_group * GROUP + k * PIECE + token

        def over(slot, total, top):
            prefix = nt_dot(query, pre_k[slot]) + mask[slot]
            span = nt_dot(query, span_k[slot])
            key_group = lax.rem(z + slot + 7, 8)
            span = jnp.where(key_group * GROUP + key_token <= query_token, span, NEG)
            new_top = jnp.maximum(
                jnp.max(prefix, axis=1, keepdims=True), jnp.max(span, axis=1, keepdims=True)
            )
            if top is not None:
                new_top = jnp.maximum(new_top, top)
            blended = nn_dot(jnp.exp2(prefix - new_top).astype(BF16), pre_v[slot])
            blended = blended + nn_dot(jnp.exp2(span - new_top).astype(BF16), span_v[slot])
            if top is not None:
                blended = blended + total * jnp.exp2(top - new_top)
            return blended, new_top

        state = over(first, None, None)
        return lax.fori_loop(first + 1, last, lambda s, c: over(s, *c), state)

    def attend_own(k):
        total, top = attend(k, 0, 0, 3)
        own_o[k] = total
        own_m[k] = jnp.broadcast_to(top, (CHUNK, HEAD))

    def attend_other(k):
        for i, (source, first) in enumerate(((1, 0), (2, 1))):
            arrive(queries.at[source, k], q_recv.at[k, i])
            total, top = attend(k, source, first, 3)
            part_o[k, i] = total[:, 0:HEAD].astype(BF16)
            part_s[k, i, 0:4, :] = jnp.transpose(jnp.broadcast_to(top, (CHUNK, HEAD)))[0:4, :]
            part_s[k, i, 4:8, :] = jnp.transpose(total[:, HEAD : 2 * HEAD])[0:4, :]
            back = device(-3 if source == 1 else 3, 0, 0)
            send(part_o.at[k, i], part_o_in.at[k, i], p_send.at[k, i, 0], p_recv.at[k, i, 0], back)
            send(part_s.at[k, i], part_s_in.at[k, i], p_send.at[k, i, 1], p_recv.at[k, i, 1], back)

    def combine(k):
        total, low, top = own_o[k][:, 0:HEAD], own_o[k][:, HEAD : 2 * HEAD], own_m[k]
        for i in range(2):
            arrive(part_o_in.at[k, i], p_recv.at[k, i, 0])
            arrive(part_s_in.at[k, i], p_recv.at[k, i, 1])
            their_top = jnp.transpose(jnp.broadcast_to(part_s_in[k, i, 0:1, :], (CHUNK, HEAD)))
            their_low = jnp.transpose(jnp.broadcast_to(part_s_in[k, i, 4:5, :], (CHUNK, HEAD)))
            new_top = jnp.maximum(top, their_top)
            mine, theirs = jnp.exp2(top - new_top), jnp.exp2(their_top - new_top)
            total = total * mine + part_o_in[k, i].astype(F32) * theirs
            low = low * mine + their_low * theirs
            top = new_top
        attended[k, :, own_cols] = (total / low).astype(BF16)
        here = attended.at[k, :, own_cols]
        send(here, here, t_send.at[k], t_recv.at[k], partner)

    first = x * other + y * core
    second = y * other + x * core

    def ring(stage, direction):
        step = 1 - 2 * direction
        along_x = other if stage == 0 else core
        return device(0, step * along_x, step * (1 - along_x))

    def chunk_rows(d):
        return slice(d * 64, (d + 1) * 64)

    def target(index, d, s):
        return lax.rem(index - 1 - s + 4, 4) if d == 0 else lax.rem(index + 1 + s, 4)

    def product(k, d, block):
        return nn_dot(attended[k, chunk_rows(d), :], o_mat[block])

    def attended_arrive(k):
        arrive(attended.at[k, :, pl.ds(pl.multiple_of(other * HEAD, HEAD), HEAD)], t_recv.at[k])

    def stage_one(k, s):
        for d in range(2):
            value = product(k, d, first if s == 3 else target(first, d, s))
            if s > 0:
                arrive(one_in.at[k, d, s - 1], one_recv.at[k, d, s - 1])
                value = value + one_in[k, d, s - 1].astype(F32)
            if s < 3:
                one_out[k, d, s] = value.astype(BF16)
                send(one_out.at[k, d, s], one_in.at[k, d, s], one_send.at[k, d, s], one_recv.at[k, d, s], ring(0, d))
            else:
                for b in range(4):
                    mid[k, d, b] = value[:, b * 256 : (b + 1) * 256]

    def stage_two(k, s):
        for d in range(2):
            value = mid[k, d, second if s == 3 else target(second, d, s)]
            if s > 0:
                arrive(two_in.at[k, d, s - 1], two_recv.at[k, d, s - 1])
                value = value + two_in[k, d, s - 1].astype(F32)
            if s < 3:
                two_out[k, d, s] = value.astype(BF16)
                send(two_out.at[k, d, s], two_in.at[k, d, s], two_send.at[k, d, s], two_recv.at[k, d, s], ring(1, d))
            else:
                result = value.astype(BF16)
                for i in range(4):
                    at = (4 * d + i) * SHARD + k * PIECE
                    out_ref[at : at + PIECE, :] = result[i * PIECE : (i + 1) * PIECE, :]

    a_mid(0)
    span_forward()
    a_mid(1)
    a_last(0)
    load_qw.wait()
    arrive(q_mat.at[:, pl.ds(pl.multiple_of(other * HEAD, HEAD), HEAD)], w_recv.at[0])
    project(0)
    a_mid(2)
    a_last(1)
    finish_queries(0)
    project(1)
    a_last(2)
    finish_queries(1)
    neighbours_arrive()
    attend_own(0)
    attend_other(0)
    project(2)
    attend_own(1)
    finish_queries(2)
    pltpu.make_async_copy(o_mat.at[:, own_cols, :], o_mat.at[:, own_cols, :], local_sems.at[5]).wait()
    arrive(o_mat.at[:, pl.ds(pl.multiple_of(other * HEAD, HEAD), HEAD), :], w_recv.at[1])
    combine(0)
    attend_other(1)
    attended_arrive(0)
    stage_one(0, 0)
    attend_own(2)
    stage_one(0, 1)
    combine(1)
    attend_other(2)
    stage_one(0, 2)
    attended_arrive(1)
    stage_one(1, 0)
    stage_one(0, 3)
    stage_two(0, 0)
    combine(2)
    stage_one(1, 1)
    stage_two(0, 1)
    attended_arrive(2)
    stage_one(2, 0)
    stage_one(1, 2)
    stage_two(0, 2)
    stage_one(2, 1)
    stage_one(1, 3)
    stage_two(1, 0)
    stage_two(0, 3)
    stage_one(2, 2)
    stage_two(1, 1)
    stage_one(2, 3)
    stage_two(2, 0)
    stage_two(1, 2)
    stage_two(2, 1)
    stage_two(1, 3)
    stage_two(2, 2)
    stage_two(2, 3)

    for copy in sent:
        copy.wait_send()
    theirs = o_mat.at[:, pl.ds(pl.multiple_of(other * HEAD, HEAD), HEAD), :]
    remote(theirs, theirs, w_send.at[1], w_recv.at[1], partner).wait_send()


def local(
    hidden, norm_gain, q_weight, q_bias, key_weight, key_bias, value_weight, value_bias, o_weight,
    cached_key_rows, cached_value_rows, keep_blocks, kept_counts, span_start,
):
    group = lax.axis_index("ctx")
    token = jnp.arange(CHUNKS * CHUNK, dtype=jnp.int32)
    token = (token % CHUNK // PIECE) * SHARD + token // CHUNK * PIECE + token % PIECE
    positions = span_start[0] + group * GROUP + token
    steps = jnp.arange(HEAD // 2, dtype=F32)
    frequency = 1000000.0 ** (-2.0 * steps / HEAD)
    angles = positions.astype(F32)[:, None] * frequency[None, :]
    cosine, sine = jnp.cos(angles), jnp.sin(angles)
    cosine = jnp.concatenate([cosine, cosine], axis=1).reshape(CHUNKS, CHUNK, HEAD)
    sine = jnp.concatenate([-sine, sine], axis=1).reshape(CHUNKS, CHUNK, HEAD)

    vmem = pl.BlockSpec(memory_space=pltpu.VMEM)
    smem = pl.BlockSpec(memory_space=pltpu.SMEM)
    hbm = pl.BlockSpec(memory_space=pl.ANY)
    dma = pltpu.SemaphoreType.DMA
    kept = jax.ShapeDtypeStruct((KEPT, HEAD), BF16)
    kept_k, kept_v, mask = pl.pallas_call(
        keep_kernel,
        out_shape=(kept, kept, jax.ShapeDtypeStruct((3, 1, KEPT), F32)),
        in_specs=[smem, smem, hbm, hbm],
        out_specs=(vmem, vmem, vmem),
        scratch_shapes=[dma((2, KEEP))],
        name="kept_blocks",
    )(keep_blocks, kept_counts, cached_key_rows, cached_value_rows)
    scratch = [
        pltpu.VMEM((SHARD, WIDTH), BF16),
        pltpu.VMEM((CHUNKS, 2, CHUNK, QUART), BF16),
        pltpu.VMEM((HALF, 2 * HEAD), BF16),
        pltpu.VMEM((WIDTH, 2 * HEAD), BF16),
        pltpu.VMEM((4, 2 * HEAD, 1024), BF16),
        pltpu.VMEM((3, KEPT, HEAD), BF16),
        pltpu.VMEM((3, KEPT, 2 * HEAD), BF16),
        pltpu.VMEM((3, GROUP, HEAD), BF16),
        pltpu.VMEM((3, GROUP, 2 * HEAD), BF16),
        pltpu.VMEM((CHUNKS, 2, CHUNK, HEAD), F32),
        pltpu.VMEM((CHUNKS, CHUNK, HEAD), F32),
        pltpu.VMEM((3, CHUNKS, CHUNK, HEAD), BF16),
        pltpu.VMEM((CHUNKS, 2, CHUNK, HEAD), BF16),
        pltpu.VMEM((CHUNKS, 2, 8, CHUNK), F32),
        pltpu.VMEM((CHUNKS, 2, CHUNK, HEAD), BF16),
        pltpu.VMEM((CHUNKS, 2, 8, CHUNK), F32),
        pltpu.VMEM((CHUNKS, CHUNK, 2 * HEAD), F32),
        pltpu.VMEM((CHUNKS, CHUNK, HEAD), F32),
        pltpu.VMEM((CHUNKS, CHUNK, 2 * HEAD), BF16),
        pltpu.VMEM((CHUNKS, 2, 3, 64, 1024), BF16),
        pltpu.VMEM((CHUNKS, 2, 3, 64, 1024), BF16),
        pltpu.VMEM((CHUNKS, 2, 4, 64, 256), F32),
        pltpu.VMEM((CHUNKS, 2, 3, 64, 256), BF16),
        pltpu.VMEM((CHUNKS, 2, 3, 64, 256), BF16),
        dma((6,)),
        dma((CHUNKS, 14)), dma((CHUNKS, 2, SHARDS)),
        dma((2,)), dma((2,)),
        dma((2, 2)), dma((2, 3)),
        dma((2, SHARDS)), dma((2, SHARDS)),
        dma((2, 2)), dma((2, 3)),
        dma((CHUNKS,)), dma((CHUNKS,)),
        dma((CHUNKS, 2)), dma((CHUNKS, 2)),
        dma((CHUNKS, 2, 2)), dma((CHUNKS, 2, 2)),
        dma((CHUNKS,)), dma((CHUNKS,)),
        dma((CHUNKS, 2, 3)), dma((CHUNKS, 2, 3)),
        dma((CHUNKS, 2, 3)), dma((CHUNKS, 2, 3)),
    ]
    return pl.pallas_call(
        kernel,
        out_shape=jax.ShapeDtypeStruct((GROUP, 256), BF16),
        in_specs=[vmem, vmem, hbm, vmem, hbm, vmem, hbm, vmem, hbm, hbm, hbm, vmem, vmem, vmem],
        out_specs=vmem,
        scratch_shapes=scratch,
        compiler_params=pltpu.CompilerParams(
            collective_id=0, has_side_effects=True, vmem_limit_bytes=56 * 1024 * 1024
        ),
        name="attention_sublayer",
    )(
        hidden, norm_gain.reshape(1, -1), q_weight, q_bias.reshape(1, -1), key_weight, key_bias.reshape(1, -1),
        value_weight, value_bias.reshape(1, -1), o_weight, kept_k, kept_v, mask, cosine, sine,
    )


def solution(mesh):
    in_specs = (
        P(("ctx", "row"), None),
        P(),
        P(None, ("head", "row")),
        P(("head", "row")),
        P(None, "head"),
        P("head"),
        P(None, "head"),
        P("head"),
        P(("head", "row"), None),
        P("ctx", "head"),
        P("ctx", "head"),
        P("ctx", None),
        P(),
        P(),
    )
    out_specs = P("ctx", ("head", "row"))
    return jax.shard_map(local, mesh=mesh, in_specs=in_specs, out_specs=out_specs, check_vma=False)
```

time: 423 us -> 103 us (0.24)
  the two profiles are of different devices: /device:TPU:1 before, /device:TPU:2 now
where the time goes in v1:
time: 103 us
  Pallas kernels  98.5 us (96%)
  local copies, waits for them, and re-layouts  2.26 us (2%)
  other arithmetic  1.71 us (2%)
    pallas_call x1, Pallas kernels, local(): pl.pallas_call(kernel, out_shape=jax.ShapeDtypeStruct((GROUP, 256), BF16)...  95.7 us
    pallas_call x1, Pallas kernels, local(): pl.pallas_call(keep_kernel, out_shape=(kept, kept, jax.ShapeDtypeStruct((...  2.75 us

profile of v1, /device:TPU:2, one launch (start us, length us, event | category | flops | bytes accessed | tf_op | source)
XLA Modules:
  0.0 103.1 jit_solution(11663967836820027011)
XLA Ops:
  0.0 0.0 copy-start
  0.7 0.8 fusion
  1.5 0.9 pad_maximum_fusion
  2.4 2.7 %kept_blocks.1 = (bf16[1024,128]{1,0:T(8,128)(2,1)}, bf16[1024,128]{1,0:T(8,128)(2,1)}, f32[3,1,1024]{2,1,0:T(1,128)}) custom-call(s32[1,8]{1,0:T(1,128)} %blocks_ref.1, s32[8]{0:T(128)} %counts_ref.1, bf16[4096,128]{1,0:T(8,128)(2,1)} %k_ref.1, bf16[4096,128]{1,0:T(8,128)(2,1)} %v_ref.1), custom_call_target="tpu_custom_call" | custom-call | tf_op jit(solution)/shard_map/kept_blocks/pallas_call | solution.py:475
  5.1 0.0 copy-done
  5.2 0.6 reshape.115.gain_ref
  5.8 95.7 %attention_sublayer.1 = bf16[384,256]{1,0:T(8,128)(2,1)} custom-call(bf16[48,8192]{1,0:T(8,128)(2,1)} %hidden_ref.1, bf16[1,8192]{1,0:T(2,128)(2,1)} %reshape.115.gain_ref, bf16[8192,128]{1,0:T(8,128)(2,1)} %qw_ref.1, bf16[1,128]{1,0:T(2,128)(2,1)} %bitcast.5, bf16[8192,128]{1,0:T(8,128)(2,1)} %kw_ref.1, bf16[1,128]{1,0:T(2,128)(2,1)} %bitcast.6, ...), custom_call_target="tpu_custom_call" | custom-call | tf_op jit(solution)/shard_map/attention_sublayer/pallas_call | solution.py:521
  101.5 1.6 %copy.17 = bf16[384,256]{1,0:T(8,128)(2,1)} copy(bf16[384,256]{1,0:T(8,128)(2,1)} %attention_sublayer.1) | data formatting | bytes 393216
  (2 shorter events, 0.0 us)
Async XLA Ops:
  0.0 5.1 %copy-start = (bf16[8192]{0:T(1024)(128)(2,1)S(1)}, bf16[8192]{0:T(1024)(128)(2,1)}, u32[]{:S(2)}) copy-start(bf16[8192]{0:T(1024)(128)(2,1)} %param.15) | copy-start | bytes 49156

commit v2 on v1

--- a/solution.py
+++ b/solution.py
@@ -127,30 +127,30 @@
 
     barrier = pltpu.get_barrier_semaphore()
     partners = [partner]
-    partners += [device(0, 1, 0), device(0, -1, 0)]
+    partners += [device(0, 1, 0), device(0, -1, 0), device(0, 2, 0)]
     partners += [row_peer(s) for s in range(1, SHARDS)]
     partners += [device(dz, 0, 0) for dz in (1, -1, 3, -3)]
     for to in partners:
         pl.semaphore_signal(barrier, inc=1, device_id=to, device_id_type=MESH)
     pl.semaphore_wait(barrier, len(partners))
 
-    total = jnp.zeros((SHARD, 1), F32)
-    for i in range(8):
-        part = hidden_ref[:, i * 1024 : (i + 1) * 1024].astype(F32)
-        total = total + jnp.sum(part * part, axis=1, keepdims=True)
-    factor = lax.rsqrt(total / WIDTH + 1e-6)
-    for i in range(8):
-        cols = slice(i * 1024, (i + 1) * 1024)
-        part = hidden_ref[:, cols].astype(F32) * factor * gain_ref[:, cols].astype(F32)
-        normed[:, cols] = part.astype(BF16)
-
     def rows_of(shard):
         return pl.ds(pl.multiple_of(shard * PIECE, PIECE), PIECE)
 
-    for k in range(CHUNKS):
+    def normalise(k):
+        rows = slice(k * PIECE, (k + 1) * PIECE)
+        total = jnp.zeros((PIECE, 1), F32)
+        for i in range(8):
+            part = hidden_ref[rows, i * 1024 : (i + 1) * 1024].astype(F32)
+            total = total + jnp.sum(part * part, axis=1, keepdims=True)
+        factor = lax.rsqrt(total / WIDTH + 1e-6)
+        for i in range(8):
+            cols = slice(i * 1024, (i + 1) * 1024)
+            part = hidden_ref[rows, cols].astype(F32) * factor * gain_ref[:, cols].astype(F32)
+            normed[rows, cols] = part.astype(BF16)
         for f in range(2):
             cols = pl.ds(pl.multiple_of(core * HALF + f * QUART, QUART), QUART)
-            gathered[k, f, rows_of(row), :] = normed[k * PIECE : (k + 1) * PIECE, cols]
+            gathered[k, f, rows_of(row), :] = normed[rows, cols]
 
     y_up, y_down = device(0, 0, 1), device(0, 0, -1)
     x_up, x_down = device(0, 1, 0), device(0, -1, 0)
@@ -196,8 +196,11 @@
         a_arrive(k, 1, far)
         forward(k, 1, far, x_down)
 
-    for k in range(CHUNKS):
-        a_start(k)
+    normalise(0)
+    a_start(0)
+    normalise(1)
+    a_start(1)
+    normalise(2)
 
     send(
         qw_ref.at[pl.ds(pl.multiple_of(other * HALF, HALF), HALF), :],
@@ -233,14 +236,17 @@
         at = pl.ds(pl.multiple_of(i * 1024, 1024), 1024)
         return total + nn_dot(normed[:, at], kv_mat[at, :])
 
-    pair = lax.fori_loop(0, 8, kv_step, jnp.zeros((SHARD, 2 * HEAD), F32))
+    def span_rows(shard):
+        return pl.ds(pl.multiple_of(shard * SHARD, SHARD), SHARD)
+
+    pair = lax.fori_loop(0, 4, kv_step, jnp.zeros((SHARD, 2 * HEAD), F32))
+    a_mid(0)
+    a_start(2)
+    pair = lax.fori_loop(4, 8, kv_step, pair)
     key_part = pair[:, 0:HEAD] + kb_ref[...].astype(F32)
     value_part = pair[:, HEAD : 2 * HEAD] + vb_ref[...].astype(F32)
     own_cos = jnp.concatenate([cos_ref[k, rows_of(row), :] for k in range(CHUNKS)], axis=0)
     own_sin = jnp.concatenate([sin_ref[k, rows_of(row), :] for k in range(CHUNKS)], axis=0)
-
-    def span_rows(shard):
-        return pl.ds(pl.multiple_of(shard * SHARD, SHARD), SHARD)
 
     span_k[1, span_rows(row), :] = rotated(key_part, own_cos, own_sin).astype(BF16)
     span_v[1, span_rows(row), 0:HEAD] = value_part.astype(BF16)
@@ -346,105 +352,90 @@
     first = x * other + y * core
     second = y * other + x * core
 
-    def ring(stage, direction):
-        step = 1 - 2 * direction
-        along_x = other if stage == 0 else core
-        return device(0, step * along_x, step * (1 - along_x))
-
-    def chunk_rows(d):
-        return slice(d * 64, (d + 1) * 64)
-
-    def target(index, d, s):
-        return lax.rem(index - 1 - s + 4, 4) if d == 0 else lax.rem(index + 1 + s, 4)
-
-    def product(k, d, block):
-        return nn_dot(attended[k, chunk_rows(d), :], o_mat[block])
+    def along(stage, ahead):
+        on_x = other if stage == 0 else core
+        return device(0, ahead * on_x, ahead * (1 - on_x))
+
+    def product(k, block):
+        return nn_dot(attended[k], o_mat[block])
 
     def attended_arrive(k):
         arrive(attended.at[k, :, pl.ds(pl.multiple_of(other * HEAD, HEAD), HEAD)], t_recv.at[k])
 
-    def stage_one(k, s):
-        for d in range(2):
-            value = product(k, d, first if s == 3 else target(first, d, s))
-            if s > 0:
-                arrive(one_in.at[k, d, s - 1], one_recv.at[k, d, s - 1])
-                value = value + one_in[k, d, s - 1].astype(F32)
-            if s < 3:
-                one_out[k, d, s] = value.astype(BF16)
-                send(one_out.at[k, d, s], one_in.at[k, d, s], one_send.at[k, d, s], one_recv.at[k, d, s], ring(0, d))
+    def stage_one(k):
+        for ahead in (2, 1, 3):
+            value = product(k, lax.rem(first + ahead, 4)).astype(BF16)
+            for b in range(4):
+                one_out[k, ahead - 1, b] = value[:, b * 256 : (b + 1) * 256]
+            at = (k, ahead - 1)
+            send(one_out.at[at], one_in.at[at], one_send.at[at], one_recv.at[at], along(0, ahead))
+        value = product(k, first)
+        for b in range(4):
+            mid[k, b] = value[:, b * 256 : (b + 1) * 256]
+
+    def stage_two(k):
+        for i in range(3):
+            arrive(one_in.at[k, i], one_recv.at[k, i])
+        for ahead in (2, 1, 3, 0):
+            b = lax.rem(second + ahead, 4)
+            value = mid[k, b]
+            for i in range(3):
+                value = value + one_in[k, i, b].astype(F32)
+            if ahead == 0:
+                mid[k, b] = value
             else:
-                for b in range(4):
-                    mid[k, d, b] = value[:, b * 256 : (b + 1) * 256]
-
-    def stage_two(k, s):
-        for d in range(2):
-            value = mid[k, d, second if s == 3 else target(second, d, s)]
-            if s > 0:
-                arrive(two_in.at[k, d, s - 1], two_recv.at[k, d, s - 1])
-                value = value + two_in[k, d, s - 1].astype(F32)
-            if s < 3:
-                two_out[k, d, s] = value.astype(BF16)
-                send(two_out.at[k, d, s], two_in.at[k, d, s], two_send.at[k, d, s], two_recv.at[k, d, s], ring(1, d))
-            else:
-                result = value.astype(BF16)
-                for i in range(4):
-                    at = (4 * d + i) * SHARD + k * PIECE
-                    out_ref[at : at + PIECE, :] = result[i * PIECE : (i + 1) * PIECE, :]
-
-    a_mid(0)
-    span_forward()
+                at = (k, ahead - 1)
+                two_out[at] = value.astype(BF16)
+                send(two_out.at[at], two_in.at[at], two_send.at[at], two_recv.at[at], along(1, ahead))
+
+    def finish(k):
+        value = mid[k, second]
+        for i in range(3):
+            arrive(two_in.at[k, i], two_recv.at[k, i])
+            value = value + two_in[k, i].astype(F32)
+        result = value.astype(BF16)
+        for i in range(SHARDS):
+            at = i * SHARD + k * PIECE
+            out_ref[at : at + PIECE, :] = result[i * PIECE : (i + 1) * PIECE, :]
+
     a_mid(1)
     a_last(0)
+    span_forward()
+    a_mid(2)
     load_qw.wait()
     arrive(q_mat.at[:, pl.ds(pl.multiple_of(other * HEAD, HEAD), HEAD)], w_recv.at[0])
     project(0)
-    a_mid(2)
     a_last(1)
     finish_queries(0)
+    a_last(2)
     project(1)
-    a_last(2)
+    neighbours_arrive()
     finish_queries(1)
-    neighbours_arrive()
     attend_own(0)
-    attend_other(0)
     project(2)
-    attend_own(1)
-    finish_queries(2)
     pltpu.make_async_copy(o_mat.at[:, own_cols, :], o_mat.at[:, own_cols, :], local_sems.at[5]).wait()
     arrive(o_mat.at[:, pl.ds(pl.multiple_of(other * HEAD, HEAD), HEAD), :], w_recv.at[1])
+    finish_queries(2)
+    attend_other(0)
+    attend_own(1)
+    attend_other(1)
+    attend_own(2)
     combine(0)
-    attend_other(1)
     attended_arrive(0)
-    stage_one(0, 0)
-    attend_own(2)
-    stage_one(0, 1)
+    stage_one(0)
+    attend_other(2)
     combine(1)
-    attend_other(2)
-    stage_one(0, 2)
     attended_arrive(1)
-    stage_one(1, 0)
-    stage_one(0, 3)
-    stage_two(0, 0)
+    stage_one(1)
+    stage_two(0)
     combine(2)
-    stage_one(1, 1)
-    stage_two(0, 1)
     attended_arrive(2)
-    stage_one(2, 0)
-    stage_one(1, 2)
-    stage_two(0, 2)
-    stage_one(2, 1)
-    stage_one(1, 3)
-    stage_two(1, 0)
-    stage_two(0, 3)
-    stage_one(2, 2)
-    stage_two(1, 1)
-    stage_one(2, 3)
-    stage_two(2, 0)
-    stage_two(1, 2)
-    stage_two(2, 1)
-    stage_two(1, 3)
-    stage_two(2, 2)
-    stage_two(2, 3)
+    stage_one(2)
+    stage_two(1)
+    finish(0)
+    stage_two(2)
+    finish(1)
+    finish(2)
 
     for copy in sent:
         copy.wait_send()
@@ -500,11 +491,11 @@
         pltpu.VMEM((CHUNKS, CHUNK, 2 * HEAD), F32),
         pltpu.VMEM((CHUNKS, CHUNK, HEAD), F32),
         pltpu.VMEM((CHUNKS, CHUNK, 2 * HEAD), BF16),
-        pltpu.VMEM((CHUNKS, 2, 3, 64, 1024), BF16),
-        pltpu.VMEM((CHUNKS, 2, 3, 64, 1024), BF16),
-        pltpu.VMEM((CHUNKS, 2, 4, 64, 256), F32),
-        pltpu.VMEM((CHUNKS, 2, 3, 64, 256), BF16),
-        pltpu.VMEM((CHUNKS, 2, 3, 64, 256), BF16),
+        pltpu.VMEM((CHUNKS, 3, 4, CHUNK, 256), BF16),
+        pltpu.VMEM((CHUNKS, 3, 4, CHUNK, 256), BF16),
+        pltpu.VMEM((CHUNKS, 4, CHUNK, 256), F32),
+        pltpu.VMEM((CHUNKS, 3, CHUNK, 256), BF16),
+        pltpu.VMEM((CHUNKS, 3, CHUNK, 256), BF16),
         dma((6,)),
         dma((CHUNKS, 14)), dma((CHUNKS, 2, SHARDS)),
         dma((2,)), dma((2,)),
@@ -515,8 +506,8 @@
         dma((CHUNKS, 2)), dma((CHUNKS, 2)),
         dma((CHUNKS, 2, 2)), dma((CHUNKS, 2, 2)),
         dma((CHUNKS,)), dma((CHUNKS,)),
-        dma((CHUNKS, 2, 3)), dma((CHUNKS, 2, 3)),
-        dma((CHUNKS, 2, 3)), dma((CHUNKS, 2, 3)),
+        dma((CHUNKS, 3)), dma((CHUNKS, 3)),
+        dma((CHUNKS, 3)), dma((CHUNKS, 3)),
     ]
     return pl.pallas_call(
         kernel,

time: 103 us -> 86.9 us (0.84)
  the two profiles are of different devices: /device:TPU:2 before, /device:TPU:1 now
where the time goes in v2:
time: 86.9 us; the launch traced here: 86.6 us
  Pallas kernels  81.9 us (94%)
  local copies, waits for them, and re-layouts  2.26 us (3%)
  other arithmetic  1.71 us (2%)
    pallas_call x1, Pallas kernels, local(): pl.pallas_call(kernel, out_shape=jax.ShapeDtypeStruct((GROUP, 256), BF16)...  79.3 us
    pallas_call x1, Pallas kernels, local(): pl.pallas_call(keep_kernel, out_shape=(kept, kept, jax.ShapeDtypeStruct((...  2.67 us

profile of v2, /device:TPU:1, one launch (start us, length us, event | category | flops | bytes accessed | tf_op | source)
XLA Modules:
  0.0 86.6 jit_solution(8335135482716436162)
XLA Ops:
  0.0 0.0 copy-start
  0.7 0.8 fusion
  1.5 0.9 %pad_maximum_fusion = (f32[3,128,128]{2,1,0:T(8,128)}, f32[3,128,128]{2,1,0:T(8,128)}) fusion(f32[3,128,64]{2,1,0:T(8,128)S(1)} %get-tuple-element.13, f32[3,128,64]{2,1,0:T(8,128)S(1)} %get-tuple-element.12, f32[3,128,64]{2,1,0:T(8,128)S(1)} %get-tuple-element.11), kind=kLoop, calls=%fused_computation.2 | loop fusion | flops 98304 | bytes 688128 | tf_op jit(solution)/shard_map/concatenate | solution.py:458
  2.4 2.7 %kept_blocks.1 = (bf16[1024,128]{1,0:T(8,128)(2,1)}, bf16[1024,128]{1,0:T(8,128)(2,1)}, f32[3,1,1024]{2,1,0:T(1,128)}) custom-call(s32[1,8]{1,0:T(1,128)} %blocks_ref.1, s32[8]{0:T(128)} %counts_ref.1, bf16[4096,128]{1,0:T(8,128)(2,1)} %k_ref.1, bf16[4096,128]{1,0:T(8,128)(2,1)} %v_ref.1), custom_call_target="tpu_custom_call" | custom-call | tf_op jit(solution)/shard_map/kept_blocks/pallas_call | solution.py:466
  5.1 0.0 copy-done
  5.1 0.6 reshape.115.gain_ref
  5.7 79.3 %attention_sublayer.1 = bf16[384,256]{1,0:T(8,128)(2,1)} custom-call(bf16[48,8192]{1,0:T(8,128)(2,1)} %hidden_ref.1, bf16[1,8192]{1,0:T(2,128)(2,1)} %reshape.115.gain_ref, bf16[8192,128]{1,0:T(8,128)(2,1)} %qw_ref.1, bf16[1,128]{1,0:T(2,128)(2,1)} %bitcast.5, bf16[8192,128]{1,0:T(8,128)(2,1)} %kw_ref.1, bf16[1,128]{1,0:T(2,128)(2,1)} %bitcast.6, ...), custom_call_target="tpu_custom_call" | custom-call | tf_op jit(solution)/shard_map/attention_sublayer/pallas_call | solution.py:512
  85.0 1.6 %copy.17 = bf16[384,256]{1,0:T(8,128)(2,1)} copy(bf16[384,256]{1,0:T(8,128)(2,1)} %attention_sublayer.1) | data formatting | bytes 393216
  (2 shorter events, 0.0 us)
Async XLA Ops:
  0.0 5.1 %copy-start = (bf16[8192]{0:T(1024)(128)(2,1)S(1)}, bf16[8192]{0:T(1024)(128)(2,1)}, u32[]{:S(2)}) copy-start(bf16[8192]{0:T(1024)(128)(2,1)} %param.15) | copy-start | bytes 49156

commit v3 on v2

--- a/solution.py
+++ b/solution.py
@@ -2,6 +2,7 @@
 
 import jax
 import jax.numpy as jnp
+import numpy as np
 from jax import lax
 from jax.experimental import pallas as pl
 from jax.experimental.pallas import tpu as pltpu
@@ -37,29 +38,12 @@
     return lax.dot_general(a, b, (((1,), (0,)), ((), ())), preferred_element_type=F32)
 
 
-def keep_kernel(blocks_ref, counts_ref, k_ref, v_ref, kept_k_ref, kept_v_ref, mask_ref, sems):
-    copies = []
-    for j in range(KEEP):
-        source = pl.ds(pl.multiple_of(blocks_ref[0, j] * BLOCK, BLOCK), BLOCK)
-        for i, (whole, kept) in enumerate(((k_ref, kept_k_ref), (v_ref, kept_v_ref))):
-            copy = pltpu.make_async_copy(whole.at[source, :], kept.at[pl.ds(j * BLOCK, BLOCK), :], sems.at[i, j])
-            copy.start()
-            copies.append(copy)
-    z = lax.axis_index("ctx")
-    for s in range(3):
-        live = counts_ref[lax.rem(z + s + 7, 8)]
-        slot = lax.broadcasted_iota(jnp.int32, (1, KEPT), 1) // BLOCK
-        mask_ref[s] = jnp.where(slot < live, 0.0, NEG).astype(F32)
-    for copy in copies:
-        copy.wait()
-
-
 def kernel(
-    hidden_ref, gain_ref, qw_ref, qb_ref, kw_ref, kb_ref, vw_ref, vb_ref, ow_ref, kept_k_ref, kept_v_ref,
-    mask, cos_ref, sin_ref,
+    hidden_ref, gain_ref, qw_ref, qb_ref, kw_ref, kb_ref, vw_ref, vb_ref, ow_ref, ck_ref, cv_ref,
+    blocks_ref, counts_ref, start_ref, freq_ref,
     out_ref,
-    normed, gathered, q_mat, kv_mat, o_mat,
-    pre_k, pre_v, span_k, span_v,
+    normed, gathered, q_mat, kv_mat, o_mat, cache_k, cache_v,
+    pre_k, pre_v, span_k, span_v, mask, cos_ref, sin_ref,
     halves, halves_in, queries, part_o, part_s, part_o_in, part_s_in,
     own_o, own_m, attended, one_out, one_in, mid, two_out, two_in,
     local_sems, a_send, a_recv, w_send, w_recv, pre_send, pre_recv, row_send, row_recv, span_send, span_recv,
@@ -105,8 +89,8 @@
         copy.start()
         return copy
 
-    load_k = load(kept_k_ref, pre_k.at[1], 0)
-    load_v = load(kept_v_ref, pre_v.at[1, :, 0:HEAD], 1)
+    load_k = load(ck_ref, cache_k, 0)
+    load_v = load(cv_ref, cache_v, 1)
     load_kw = load(kw_ref, kv_mat.at[:, 0:HEAD], 2)
     load_vw = load(vw_ref, kv_mat.at[:, HEAD : 2 * HEAD], 3)
     own_cols = pl.ds(pl.multiple_of(core * HEAD, HEAD), HEAD)
@@ -146,7 +130,7 @@
         factor = lax.rsqrt(total / WIDTH + 1e-6)
         for i in range(8):
             cols = slice(i * 1024, (i + 1) * 1024)
-            part = hidden_ref[rows, cols].astype(F32) * factor * gain_ref[:, cols].astype(F32)
+            part = hidden_ref[rows, cols].astype(F32) * factor * gain_ref[cols].astype(F32).reshape(1, 1024)
             normed[rows, cols] = part.astype(BF16)
         for f in range(2):
             cols = pl.ds(pl.multiple_of(core * HALF + f * QUART, QUART), QUART)
@@ -206,45 +190,56 @@
         qw_ref.at[pl.ds(pl.multiple_of(other * HALF, HALF), HALF), :],
         q_mat.at[:, own_cols], w_send.at[0], w_recv.at[0], partner,
     )
-    for b1 in range(4):
-        for b2 in range(4):
-            remote(
-                ow_ref.at[:, pl.ds(column(other, b1, b2), 256)],
-                o_mat.at[b1, own_cols, pl.ds(b2 * 256, 256)],
-                w_send.at[1], w_recv.at[1], partner,
-            ).start()
-
     load_k.wait()
     load_v.wait()
+    for j in range(KEEP):
+        pre_k[1, j * BLOCK : (j + 1) * BLOCK, :] = cache_k[blocks_ref[0, j]]
+        pre_v[1, j * BLOCK : (j + 1) * BLOCK, 0:HEAD] = cache_v[blocks_ref[0, j]]
     z_up, z_down = device(1, 0, 0), device(-1, 0, 0)
     left = pl.ds(0, HEAD)
+    for s in range(3):
+        pre_v[s, :, HEAD : 2 * HEAD] = jnp.ones((KEPT, HEAD), BF16)
+        span_v[s, :, HEAD : 2 * HEAD] = jnp.ones((GROUP, HEAD), BF16)
+        live = counts_ref[lax.rem(z + s + 7, N_CTX)]
+        slot_index = lax.broadcasted_iota(jnp.int32, (1, KEPT), 1) // BLOCK
+        mask[s] = jnp.where(slot_index < live, 0.0, NEG).astype(F32)
+
+    token = lax.broadcasted_iota(jnp.int32, (CHUNK, 1), 0)
+    token = (token // PIECE) * SHARD + lax.rem(token, PIECE)
+    sign = jnp.where(lax.broadcasted_iota(jnp.int32, (1, HEAD), 1) < HEAD // 2, -1.0, 1.0)
+
+    def angles_of(k):
+        positions = (start_ref[0] + z * GROUP + k * PIECE + token).astype(F32)
+        angles = positions * freq_ref[...]
+        cos_ref[k] = jnp.cos(angles)
+        sin_ref[k] = jnp.sin(angles) * sign
+
+    for k in range(CHUNKS):
+        angles_of(k)
+
+    def rotated(values, cosine, sine):
+        return values * cosine + pltpu.roll(values, HEAD // 2, 1) * sine
+
+    load_kw.wait()
+    load_vw.wait()
+
+    def kv_step(i, total):
+        at = pl.ds(pl.multiple_of(i * 1024, 1024), 1024)
+        return total + nn_dot(normed[:, at], kv_mat[at, :])
+
+    def span_rows(shard):
+        return pl.ds(pl.multiple_of(shard * SHARD, SHARD), SHARD)
+
+    pair = lax.fori_loop(0, 4, kv_step, jnp.zeros((SHARD, 2 * HEAD), F32))
+    a_mid(0)
+    a_start(2)
     for i, (slot, to) in enumerate(((0, z_up), (2, z_down))):
         send(pre_k.at[1], pre_k.at[slot], pre_send.at[0, i], pre_recv.at[0, slot], to)
         send(pre_v.at[1, :, left], pre_v.at[slot, :, left], pre_send.at[1, i], pre_recv.at[1, slot], to)
 
-    for s in range(3):
-        pre_v[s, :, HEAD : 2 * HEAD] = jnp.ones((KEPT, HEAD), BF16)
-        span_v[s, :, HEAD : 2 * HEAD] = jnp.ones((GROUP, HEAD), BF16)
-
-    def rotated(values, cosine, sine):
-        return values * cosine + pltpu.roll(values, HEAD // 2, 1) * sine
-
-    load_kw.wait()
-    load_vw.wait()
-
-    def kv_step(i, total):
-        at = pl.ds(pl.multiple_of(i * 1024, 1024), 1024)
-        return total + nn_dot(normed[:, at], kv_mat[at, :])
-
-    def span_rows(shard):
-        return pl.ds(pl.multiple_of(shard * SHARD, SHARD), SHARD)
-
-    pair = lax.fori_loop(0, 4, kv_step, jnp.zeros((SHARD, 2 * HEAD), F32))
-    a_mid(0)
-    a_start(2)
     pair = lax.fori_loop(4, 8, kv_step, pair)
-    key_part = pair[:, 0:HEAD] + kb_ref[...].astype(F32)
-    value_part = pair[:, HEAD : 2 * HEAD] + vb_ref[...].astype(F32)
+    key_part = pair[:, 0:HEAD] + kb_ref[...].astype(F32).reshape(1, HEAD)
+    value_part = pair[:, HEAD : 2 * HEAD] + vb_ref[...].astype(F32).reshape(1, HEAD)
     own_cos = jnp.concatenate([cos_ref[k, rows_of(row), :] for k in range(CHUNKS)], axis=0)
     own_sin = jnp.concatenate([sin_ref[k, rows_of(row), :] for k in range(CHUNKS)], axis=0)
 
@@ -283,14 +278,12 @@
 
     def finish_queries(k):
         arrive(halves_in.at[k], h_recv.at[k])
-        values = halves[k, core] + halves_in[k] + qb_ref[...].astype(F32)
+        values = halves[k, core] + halves_in[k] + qb_ref[...].astype(F32).reshape(1, HEAD)
         values = rotated(values, cos_ref[k], sin_ref[k]) * (LOG2E / math.sqrt(HEAD))
         queries[0, k] = values.astype(BF16)
         send(queries.at[0, k], queries.at[1, k], q_send.at[k, 0], q_recv.at[k, 0], device(3, 0, 0))
         send(queries.at[0, k], queries.at[2, k], q_send.at[k, 1], q_recv.at[k, 1], device(-3, 0, 0))
 
-    token = lax.broadcasted_iota(jnp.int32, (CHUNK, 1), 0)
-    token = (token // PIECE) * SHARD + lax.rem(token, PIECE)
     key_token = lax.broadcasted_iota(jnp.int32, (1, GROUP), 1)
 
     def attend(k, source, first, last):
@@ -408,6 +401,14 @@
     a_last(1)
     finish_queries(0)
     a_last(2)
+    for b1 in range(4):
+        for b2 in range(4):
+            remote(
+                ow_ref.at[:, pl.ds(column(other, b1, b2), 256)],
+                o_mat.at[b1, own_cols, pl.ds(b2 * 256, 256)],
+                w_send.at[1], w_recv.at[1], partner,
+            ).start()
+
     project(1)
     neighbours_arrive()
     finish_queries(1)
@@ -447,40 +448,29 @@
     hidden, norm_gain, q_weight, q_bias, key_weight, key_bias, value_weight, value_bias, o_weight,
     cached_key_rows, cached_value_rows, keep_blocks, kept_counts, span_start,
 ):
-    group = lax.axis_index("ctx")
-    token = jnp.arange(CHUNKS * CHUNK, dtype=jnp.int32)
-    token = (token % CHUNK // PIECE) * SHARD + token // CHUNK * PIECE + token % PIECE
-    positions = span_start[0] + group * GROUP + token
-    steps = jnp.arange(HEAD // 2, dtype=F32)
-    frequency = 1000000.0 ** (-2.0 * steps / HEAD)
-    angles = positions.astype(F32)[:, None] * frequency[None, :]
-    cosine, sine = jnp.cos(angles), jnp.sin(angles)
-    cosine = jnp.concatenate([cosine, cosine], axis=1).reshape(CHUNKS, CHUNK, HEAD)
-    sine = jnp.concatenate([-sine, sine], axis=1).reshape(CHUNKS, CHUNK, HEAD)
+    steps = np.arange(HEAD // 2, dtype=np.float64)
+    frequency = (1000000.0 ** (-2.0 * steps / HEAD)).astype(np.float32)
+    frequency = np.concatenate([frequency, frequency])[None, :]
 
     vmem = pl.BlockSpec(memory_space=pltpu.VMEM)
     smem = pl.BlockSpec(memory_space=pltpu.SMEM)
     hbm = pl.BlockSpec(memory_space=pl.ANY)
     dma = pltpu.SemaphoreType.DMA
-    kept = jax.ShapeDtypeStruct((KEPT, HEAD), BF16)
-    kept_k, kept_v, mask = pl.pallas_call(
-        keep_kernel,
-        out_shape=(kept, kept, jax.ShapeDtypeStruct((3, 1, KEPT), F32)),
-        in_specs=[smem, smem, hbm, hbm],
-        out_specs=(vmem, vmem, vmem),
-        scratch_shapes=[dma((2, KEEP))],
-        name="kept_blocks",
-    )(keep_blocks, kept_counts, cached_key_rows, cached_value_rows)
     scratch = [
         pltpu.VMEM((SHARD, WIDTH), BF16),
         pltpu.VMEM((CHUNKS, 2, CHUNK, QUART), BF16),
         pltpu.VMEM((HALF, 2 * HEAD), BF16),
         pltpu.VMEM((WIDTH, 2 * HEAD), BF16),
         pltpu.VMEM((4, 2 * HEAD, 1024), BF16),
+        pltpu.VMEM((32, BLOCK, HEAD), BF16),
+        pltpu.VMEM((32, BLOCK, HEAD), BF16),
         pltpu.VMEM((3, KEPT, HEAD), BF16),
         pltpu.VMEM((3, KEPT, 2 * HEAD), BF16),
         pltpu.VMEM((3, GROUP, HEAD), BF16),
         pltpu.VMEM((3, GROUP, 2 * HEAD), BF16),
+        pltpu.VMEM((3, 1, KEPT), F32),
+        pltpu.VMEM((CHUNKS, CHUNK, HEAD), F32),
+        pltpu.VMEM((CHUNKS, CHUNK, HEAD), F32),
         pltpu.VMEM((CHUNKS, 2, CHUNK, HEAD), F32),
         pltpu.VMEM((CHUNKS, CHUNK, HEAD), F32),
         pltpu.VMEM((3, CHUNKS, CHUNK, HEAD), BF16),
@@ -512,7 +502,7 @@
     return pl.pallas_call(
         kernel,
         out_shape=jax.ShapeDtypeStruct((GROUP, 256), BF16),
-        in_specs=[vmem, vmem, hbm, vmem, hbm, vmem, hbm, vmem, hbm, hbm, hbm, vmem, vmem, vmem],
+        in_specs=[vmem, vmem, hbm, vmem, hbm, vmem, hbm, vmem, hbm, hbm, hbm, smem, smem, smem, vmem],
         out_specs=vmem,
         scratch_shapes=scratch,
         compiler_params=pltpu.CompilerParams(
@@ -520,8 +510,9 @@
         ),
         name="attention_sublayer",
     )(
-        hidden, norm_gain.reshape(1, -1), q_weight, q_bias.reshape(1, -1), key_weight, key_bias.reshape(1, -1),
-        value_weight, value_bias.reshape(1, -1), o_weight, kept_k, kept_v, mask, cosine, sine,
+        hidden, norm_gain, q_weight, q_bias, key_weight, key_bias, value_weight, value_bias, o_weight,
+        cached_key_rows.reshape(32, BLOCK, HEAD), cached_value_rows.reshape(32, BLOCK, HEAD),
+        keep_blocks, kept_counts, span_start, jnp.asarray(frequency),
     )
 
 

time: 86.9 us -> 81.7 us (0.940)
  Pallas kernels: 81.9 us -> 79.3 us
  other arithmetic: 1.71 us -> 0 us
    pallas_call x1 -> x0, Pallas kernels: 2.67 us -> none  [local(): pl.pallas_call(keep_kernel, out_shape=(kept, kept, jax.ShapeDtypeStruct((...]
    concatenate x1 -> x0, other arithmetic: 0.91 us -> none  [local(): jnp.concatenate([cosine, cosine], axis=1).reshape(CHUNKS, CHUNK, HEAD)]
where the time goes in v3:
time: 81.7 us; the launch traced here: 81.6 us
  Pallas kernels  79.3 us (97%)
  local copies, waits for them, and re-layouts  1.62 us (2%)
    pallas_call x1, Pallas kernels, local(): pl.pallas_call(kernel, out_shape=jax.ShapeDtypeStruct((GROUP, 256), BF16)...  79.3 us

profile of v3, /device:TPU:1, one launch (start us, length us, event | category | flops | bytes accessed | tf_op | source)
XLA Modules:
  0.0 81.6 jit_solution(4570181716242241137)
XLA Ops:
  0.7 79.3 %attention_sublayer.1 = bf16[384,256]{1,0:T(8,128)(2,1)} custom-call(bf16[48,8192]{1,0:T(8,128)(2,1)} %hidden_ref.1, bf16[8192]{0:T(1024)(128)(2,1)} %gain_ref.1, bf16[8192,128]{1,0:T(8,128)(2,1)} %qw_ref.1, bf16[128]{0:T(256)(128)(2,1)} %qb_ref.1, bf16[8192,128]{1,0:T(8,128)(2,1)} %kw_ref.1, bf16[128]{0:T(256)(128)(2,1)} %kb_ref.1, ...), custom_call_target="tpu_custom_call" | custom-call | tf_op jit(solution)/shard_map/attention_sublayer/pallas_call | solution.py:502
  80.0 1.6 %copy.18 = bf16[384,256]{1,0:T(8,128)(2,1)} copy(bf16[384,256]{1,0:T(8,128)(2,1)} %attention_sublayer.1) | data formatting | bytes 393216

commit v4 on v3

--- a/solution.py
+++ b/solution.py
@@ -45,9 +45,9 @@
     normed, gathered, q_mat, kv_mat, o_mat, cache_k, cache_v,
     pre_k, pre_v, span_k, span_v, mask, cos_ref, sin_ref,
     halves, halves_in, queries, part_o, part_s, part_o_in, part_s_in,
-    own_o, own_m, attended, one_out, one_in, mid, two_out, two_in,
-    local_sems, a_send, a_recv, w_send, w_recv, pre_send, pre_recv, row_send, row_recv, span_send, span_recv,
-    h_send, h_recv, q_send, q_recv, p_send, p_recv, t_send, t_recv, one_send, one_recv, two_send, two_recv,
+    own_o, own_m, own_head, attended, one_out, one_in, mid,
+    local_sems, a_send, a_recv, w_send, w_recv, o_recv, pre_send, pre_recv, row_send, row_recv, span_send, span_recv,
+    h_send, h_recv, q_send, q_recv, p_send, p_recv, t_send, t_recv, one_send, one_recv,
 ):
     z = lax.axis_index("ctx")
     head = lax.axis_index("head")
@@ -96,23 +96,33 @@
     own_cols = pl.ds(pl.multiple_of(core * HEAD, HEAD), HEAD)
     load_qw = load(qw_ref.at[pl.ds(pl.multiple_of(core * HALF, HALF), HALF), :], q_mat.at[:, own_cols], 4)
 
-    def column(cc, first, second):
-        xx = first * (1 - cc) + second * cc
-        yy = second * (1 - cc) + first * cc
-        return pl.multiple_of((2 * (xx // 2) + cc) * 2048 + (4 * lax.rem(xx, 2) + yy) * 256, 256)
-
-    for b1 in range(4):
-        for b2 in range(4):
-            pltpu.make_async_copy(
-                ow_ref.at[:, pl.ds(column(core, b1, b2), 256)],
-                o_mat.at[b1, own_cols, pl.ds(b2 * 256, 256)],
-                local_sems.at[5],
-            ).start()
+    def gather_place(cc):
+        return y * (1 - cc) + x * cc
+
+    def columns(cc, summed, place):
+        xx = summed * (1 - cc) + place * cc
+        yy = place * (1 - cc) + summed * cc
+        return pl.ds(pl.multiple_of((2 * (xx // 2) + cc) * 2048 + (4 * lax.rem(xx, 2) + yy) * 256, 256), 256)
+
+    def head_slot(cc):
+        return 2 * gather_place(cc) + core
+
+    def slot_of(index):
+        return pl.ds(pl.multiple_of(index * HEAD, HEAD), HEAD)
+
+    for q in range(4):
+        pltpu.make_async_copy(
+            ow_ref.at[:, columns(core, q, gather_place(core))],
+            o_mat.at[slot_of(head_slot(core)), pl.ds(q * 256, 256)],
+            local_sems.at[5],
+        ).start()
 
     barrier = pltpu.get_barrier_semaphore()
     partners = [partner]
-    partners += [device(0, 1, 0), device(0, -1, 0), device(0, 2, 0)]
-    partners += [row_peer(s) for s in range(1, SHARDS)]
+    partners += [device(0, s, 0, c) for s in range(1, 4) for c in range(2)]
+    partners += [device(0, 0, s, c) for s in range(1, 4) for c in range(2)]
+    beside = 4 * (1 - x_lo)
+    partners += [(z, head, beside + lax.rem(y + s, 4)) for s in range(1, 4)]
     partners += [device(dz, 0, 0) for dz in (1, -1, 3, -3)]
     for to in partners:
         pl.semaphore_signal(barrier, inc=1, device_id=to, device_id_type=MESH)
@@ -338,54 +348,62 @@
             total = total * mine + part_o_in[k, i].astype(F32) * theirs
             low = low * mine + their_low * theirs
             top = new_top
-        attended[k, :, own_cols] = (total / low).astype(BF16)
-        here = attended.at[k, :, own_cols]
-        send(here, here, t_send.at[k], t_recv.at[k], partner)
-
-    first = x * other + y * core
-    second = y * other + x * core
-
-    def along(stage, ahead):
-        on_x = other if stage == 0 else core
-        return device(0, ahead * on_x, ahead * (1 - on_x))
-
-    def product(k, block):
-        return nn_dot(attended[k], o_mat[block])
-
-    def attended_arrive(k):
-        arrive(attended.at[k, :, pl.ds(pl.multiple_of(other * HEAD, HEAD), HEAD)], t_recv.at[k])
+        result = (total / low).astype(BF16)
+        own_head[k] = result
+        attended[k, :, slot_of(head_slot(core))] = result
+        for i, (cc, to) in enumerate(gatherers):
+            slot = head_slot(cc)
+            send(own_head.at[k], attended.at[k, :, slot_of(slot)], t_send.at[k, i], t_recv.at[k, slot], to)
+
+    gatherers = [(0, device(0, 0, s, 0)) for s in (2, 1, 3)] + [(1, device(0, s, 0, 1)) for s in (2, 1, 3)]
+    gatherers += [(other, partner)]
+    gather_at, sum_at = gather_place(core), x * other + y * core
+
+    def send_o_weight():
+        for i, (cc, to) in enumerate(gatherers):
+            if i < 6:
+                ahead = (2, 1, 3)[i % 3]
+                place = lax.rem((y if cc == 0 else x) + ahead, 4)
+            else:
+                place = gather_place(cc)
+            for q in range(4):
+                remote(
+                    ow_ref.at[:, columns(cc, q, place)],
+                    o_mat.at[slot_of(head_slot(cc)), pl.ds(q * 256, 256)],
+                    w_send.at[1 + i], o_recv.at[head_slot(cc)], to,
+                ).start()
+
+    def other_heads(do):
+        for ahead in range(1, 4):
+            for c in range(2):
+                do(2 * lax.rem(gather_at + ahead, 4) + c)
+        do(2 * gather_at + other)
+
+    def o_weight_arrive():
+        own = o_mat.at[slot_of(head_slot(core)), :]
+        pltpu.make_async_copy(own, own, local_sems.at[5]).wait()
+        other_heads(lambda slot: arrive(o_mat.at[slot_of(slot), :], o_recv.at[slot]))
+
+    def along(ahead):
+        return device(0, ahead * other, ahead * core)
 
     def stage_one(k):
-        for ahead in (2, 1, 3):
-            value = product(k, lax.rem(first + ahead, 4)).astype(BF16)
-            for b in range(4):
-                one_out[k, ahead - 1, b] = value[:, b * 256 : (b + 1) * 256]
-            at = (k, ahead - 1)
-            send(one_out.at[at], one_in.at[at], one_send.at[at], one_recv.at[at], along(0, ahead))
-        value = product(k, first)
-        for b in range(4):
-            mid[k, b] = value[:, b * 256 : (b + 1) * 256]
-
-    def stage_two(k):
+        other_heads(lambda slot: arrive(attended.at[k, :, slot_of(slot)], t_recv.at[k, slot]))
+        for ahead in (2, 1, 3, 0):
+            target = pl.ds(pl.multiple_of(lax.rem(sum_at + ahead, 4) * 256, 256), 256)
+            value = nn_dot(attended[k], o_mat[:, target])
+            if ahead == 0:
+                mid[k] = value
+            else:
+                at = (k, ahead - 1)
+                one_out[at] = value.astype(BF16)
+                send(one_out.at[at], one_in.at[at], one_send.at[at], one_recv.at[at], along(ahead))
+
+    def finish(k):
+        value = mid[k]
         for i in range(3):
             arrive(one_in.at[k, i], one_recv.at[k, i])
-        for ahead in (2, 1, 3, 0):
-            b = lax.rem(second + ahead, 4)
-            value = mid[k, b]
-            for i in range(3):
-                value = value + one_in[k, i, b].astype(F32)
-            if ahead == 0:
-                mid[k, b] = value
-            else:
-                at = (k, ahead - 1)
-                two_out[at] = value.astype(BF16)
-                send(two_out.at[at], two_in.at[at], two_send.at[at], two_recv.at[at], along(1, ahead))
-
-    def finish(k):
-        value = mid[k, second]
-        for i in range(3):
-            arrive(two_in.at[k, i], two_recv.at[k, i])
-            value = value + two_in[k, i].astype(F32)
+            value = value + one_in[k, i].astype(F32)
         result = value.astype(BF16)
         for i in range(SHARDS):
             at = i * SHARD + k * PIECE
@@ -401,47 +419,34 @@
     a_last(1)
     finish_queries(0)
     a_last(2)
-    for b1 in range(4):
-        for b2 in range(4):
-            remote(
-                ow_ref.at[:, pl.ds(column(other, b1, b2), 256)],
-                o_mat.at[b1, own_cols, pl.ds(b2 * 256, 256)],
-                w_send.at[1], w_recv.at[1], partner,
-            ).start()
-
+    send_o_weight()
     project(1)
     neighbours_arrive()
     finish_queries(1)
     attend_own(0)
     project(2)
-    pltpu.make_async_copy(o_mat.at[:, own_cols, :], o_mat.at[:, own_cols, :], local_sems.at[5]).wait()
-    arrive(o_mat.at[:, pl.ds(pl.multiple_of(other * HEAD, HEAD), HEAD), :], w_recv.at[1])
     finish_queries(2)
     attend_other(0)
     attend_own(1)
     attend_other(1)
     attend_own(2)
     combine(0)
-    attended_arrive(0)
+    attend_other(2)
+    o_weight_arrive()
     stage_one(0)
-    attend_other(2)
     combine(1)
-    attended_arrive(1)
     stage_one(1)
-    stage_two(0)
     combine(2)
-    attended_arrive(2)
+    finish(0)
     stage_one(2)
-    stage_two(1)
-    finish(0)
-    stage_two(2)
     finish(1)
     finish(2)
 
     for copy in sent:
         copy.wait_send()
-    theirs = o_mat.at[:, pl.ds(pl.multiple_of(other * HEAD, HEAD), HEAD), :]
-    remote(theirs, theirs, w_send.at[1], w_recv.at[1], partner).wait_send()
+    for i in range(7):
+        piece = o_mat.at[slot_of(i), :]
+        remote(piece, piece, w_send.at[1 + i], o_recv.at[i], partner).wait_send()
 
 
 def local(
@@ -461,7 +466,7 @@
         pltpu.VMEM((CHUNKS, 2, CHUNK, QUART), BF16),
         pltpu.VMEM((HALF, 2 * HEAD), BF16),
         pltpu.VMEM((WIDTH, 2 * HEAD), BF16),
-        pltpu.VMEM((4, 2 * HEAD, 1024), BF16),
+        pltpu.VMEM((8 * HEAD, 1024), BF16),
         pltpu.VMEM((32, BLOCK, HEAD), BF16),
         pltpu.VMEM((32, BLOCK, HEAD), BF16),
         pltpu.VMEM((3, KEPT, HEAD), BF16),
@@ -480,23 +485,21 @@
         pltpu.VMEM((CHUNKS, 2, 8, CHUNK), F32),
         pltpu.VMEM((CHUNKS, CHUNK, 2 * HEAD), F32),
         pltpu.VMEM((CHUNKS, CHUNK, HEAD), F32),
-        pltpu.VMEM((CHUNKS, CHUNK, 2 * HEAD), BF16),
-        pltpu.VMEM((CHUNKS, 3, 4, CHUNK, 256), BF16),
-        pltpu.VMEM((CHUNKS, 3, 4, CHUNK, 256), BF16),
-        pltpu.VMEM((CHUNKS, 4, CHUNK, 256), F32),
+        pltpu.VMEM((CHUNKS, CHUNK, HEAD), BF16),
+        pltpu.VMEM((CHUNKS, CHUNK, 8 * HEAD), BF16),
         pltpu.VMEM((CHUNKS, 3, CHUNK, 256), BF16),
         pltpu.VMEM((CHUNKS, 3, CHUNK, 256), BF16),
+        pltpu.VMEM((CHUNKS, CHUNK, 256), F32),
         dma((6,)),
         dma((CHUNKS, 14)), dma((CHUNKS, 2, SHARDS)),
-        dma((2,)), dma((2,)),
+        dma((8,)), dma((1,)), dma((8,)),
         dma((2, 2)), dma((2, 3)),
         dma((2, SHARDS)), dma((2, SHARDS)),
         dma((2, 2)), dma((2, 3)),
         dma((CHUNKS,)), dma((CHUNKS,)),
         dma((CHUNKS, 2)), dma((CHUNKS, 2)),
         dma((CHUNKS, 2, 2)), dma((CHUNKS, 2, 2)),
-        dma((CHUNKS,)), dma((CHUNKS,)),
-        dma((CHUNKS, 3)), dma((CHUNKS, 3)),
+        dma((CHUNKS, 7)), dma((CHUNKS, 8)),
         dma((CHUNKS, 3)), dma((CHUNKS, 3)),
     ]
     return pl.pallas_call(

time: 81.7 us -> 77.7 us (0.951)
  Pallas kernels: 79.3 us -> 75.3 us
    pallas_call x1, Pallas kernels: 79.3 us -> 75.3 us  [local(): pl.pallas_call(kernel, out_shape=jax.ShapeDtypeStruct((GROUP, 256), BF16)...]
where the time goes in v4:
time: 77.7 us; the launch traced here: 77.6 us
  Pallas kernels  75.3 us (97%)
  local copies, waits for them, and re-layouts  1.62 us (2%)
    pallas_call x1, Pallas kernels, local(): pl.pallas_call(kernel, out_shape=jax.ShapeDtypeStruct((GROUP, 256), BF16)...  75.3 us
    unnamed x1, local copies, waits for them, and re-layouts  1.62 us

profile of v4, /device:TPU:1, one launch (start us, length us, event | category | flops | bytes accessed | tf_op | source)
XLA Modules:
  0.0 77.6 jit_solution(18380298863931712681)
XLA Ops:
  0.7 75.3 %attention_sublayer.1 = bf16[384,256]{1,0:T(8,128)(2,1)} custom-call(bf16[48,8192]{1,0:T(8,128)(2,1)} %hidden_ref.1, bf16[8192]{0:T(1024)(128)(2,1)} %gain_ref.1, bf16[8192,128]{1,0:T(8,128)(2,1)} %qw_ref.1, bf16[128]{0:T(256)(128)(2,1)} %qb_ref.1, bf16[8192,128]{1,0:T(8,128)(2,1)} %kw_ref.1, bf16[128]{0:T(256)(128)(2,1)} %kb_ref.1, ...), custom_call_target="tpu_custom_call" | custom-call | tf_op jit(solution)/shard_map/attention_sublayer/pallas_call | solution.py:505
  75.9 1.6 %copy.18 = bf16[384,256]{1,0:T(8,128)(2,1)} copy(bf16[384,256]{1,0:T(8,128)(2,1)} %attention_sublayer.1) | data formatting | bytes 393216

commit v5 on v4

--- a/solution.py
+++ b/solution.py
@@ -126,7 +126,6 @@
     partners += [device(dz, 0, 0) for dz in (1, -1, 3, -3)]
     for to in partners:
         pl.semaphore_signal(barrier, inc=1, device_id=to, device_id_type=MESH)
-    pl.semaphore_wait(barrier, len(partners))
 
     def rows_of(shard):
         return pl.ds(pl.multiple_of(shard * PIECE, PIECE), PIECE)
@@ -191,10 +190,11 @@
         forward(k, 1, far, x_down)
 
     normalise(0)
+    normalise(1)
+    normalise(2)
+    pl.semaphore_wait(barrier, len(partners))
     a_start(0)
-    normalise(1)
     a_start(1)
-    normalise(2)
 
     send(
         qw_ref.at[pl.ds(pl.multiple_of(other * HALF, HALF), HALF), :],
@@ -296,45 +296,67 @@
 
     key_token = lax.broadcasted_iota(jnp.int32, (1, GROUP), 1)
 
-    def attend(k, source, first, last):
-        query = queries[source, k]
-        query_group = lax.rem(z + (0, 5, 3)[source], 8)
-        query_token = query_group * GROUP + k * PIECE + token
-
-        def over(slot, total, top):
-            prefix = nt_dot(query, pre_k[slot]) + mask[slot]
-            span = nt_dot(query, span_k[slot])
-            key_group = lax.rem(z + slot + 7, 8)
-            span = jnp.where(key_group * GROUP + key_token <= query_token, span, NEG)
-            new_top = jnp.maximum(
-                jnp.max(prefix, axis=1, keepdims=True), jnp.max(span, axis=1, keepdims=True)
-            )
-            if top is not None:
-                new_top = jnp.maximum(new_top, top)
-            blended = nn_dot(jnp.exp2(prefix - new_top).astype(BF16), pre_v[slot])
-            blended = blended + nn_dot(jnp.exp2(span - new_top).astype(BF16), span_v[slot])
-            if top is not None:
-                blended = blended + total * jnp.exp2(top - new_top)
-            return blended, new_top
-
-        state = over(first, None, None)
-        return lax.fori_loop(first + 1, last, lambda s, c: over(s, *c), state)
-
-    def attend_own(k):
-        total, top = attend(k, 0, 0, 3)
-        own_o[k] = total
-        own_m[k] = jnp.broadcast_to(top, (CHUNK, HEAD))
-
-    def attend_other(k):
+    def tokens_of(source, chunks):
+        group = lax.rem(z + (0, 5, 3)[source], N_CTX)
+        return jnp.concatenate([group * GROUP + k * PIECE + token for k in chunks], axis=0)
+
+    def over(query, query_token, slot, total, top):
+        prefix = nt_dot(query, pre_k[slot]) + mask[slot]
+        span = nt_dot(query, span_k[slot])
+        key_group = lax.rem(z + slot + 7, N_CTX)
+        span = jnp.where(key_group * GROUP + key_token <= query_token, span, NEG)
+        new_top = jnp.maximum(jnp.max(prefix, axis=1, keepdims=True), jnp.max(span, axis=1, keepdims=True))
+        if top is not None:
+            new_top = jnp.maximum(new_top, top)
+        blended = nn_dot(jnp.exp2(prefix - new_top).astype(BF16), pre_v[slot])
+        blended = blended + nn_dot(jnp.exp2(span - new_top).astype(BF16), span_v[slot])
+        if top is not None:
+            blended = blended + total * jnp.exp2(top - new_top)
+        return blended, new_top
+
+    def attend(query, query_token, first):
+        state = over(query, query_token, first, None, None)
+        return lax.fori_loop(first + 1, 3, lambda s, c: over(query, query_token, s, *c), state)
+
+    def attend_own():
+        total, top = attend(queries[0].reshape(GROUP, HEAD), tokens_of(0, range(CHUNKS)), 0)
+        for k in range(CHUNKS):
+            rows = slice(k * CHUNK, (k + 1) * CHUNK)
+            own_o[k] = total[rows]
+            own_m[k] = jnp.broadcast_to(top[rows], (CHUNK, HEAD))
+
+    def give_back(k, i, total, top):
+        part_o[k, i] = total[:, 0:HEAD].astype(BF16)
+        part_s[k, i, 0:4, :] = jnp.transpose(jnp.broadcast_to(top, (CHUNK, HEAD)))[0:4, :]
+        part_s[k, i, 4:8, :] = jnp.transpose(total[:, HEAD : 2 * HEAD])[0:4, :]
+        back = device((-3, 3)[i], 0, 0)
+        send(part_o.at[k, i], part_o_in.at[k, i], p_send.at[k, i, 0], p_recv.at[k, i, 0], back)
+        send(part_s.at[k, i], part_s_in.at[k, i], p_send.at[k, i, 1], p_recv.at[k, i, 1], back)
+
+    def attend_early():
         for i, (source, first) in enumerate(((1, 0), (2, 1))):
-            arrive(queries.at[source, k], q_recv.at[k, i])
-            total, top = attend(k, source, first, 3)
-            part_o[k, i] = total[:, 0:HEAD].astype(BF16)
-            part_s[k, i, 0:4, :] = jnp.transpose(jnp.broadcast_to(top, (CHUNK, HEAD)))[0:4, :]
-            part_s[k, i, 4:8, :] = jnp.transpose(total[:, HEAD : 2 * HEAD])[0:4, :]
-            back = device(-3 if source == 1 else 3, 0, 0)
-            send(part_o.at[k, i], part_o_in.at[k, i], p_send.at[k, i, 0], p_recv.at[k, i, 0], back)
-            send(part_s.at[k, i], part_s_in.at[k, i], p_send.at[k, i, 1], p_recv.at[k, i, 1], back)
+            for k in range(2):
+                arrive(queries.at[source, k], q_recv.at[k, i])
+            query = queries[source, 0:2].reshape(2 * CHUNK, HEAD)
+            total, top = attend(query, tokens_of(source, range(2)), first)
+            for k in range(2):
+                rows = slice(k * CHUNK, (k + 1) * CHUNK)
+                give_back(k, i, total[rows], top[rows])
+
+    def attend_last():
+        arrive(queries.at[1, 2], q_recv.at[2, 0])
+        arrive(queries.at[2, 2], q_recv.at[2, 1])
+        below, above = tokens_of(1, (2,)), tokens_of(2, (2,))
+        total, top = over(queries[1, 2], below, 0, None, None)
+        query = jnp.concatenate([queries[1, 2], queries[2, 2]], axis=0)
+        query_token = jnp.concatenate([below, above], axis=0)
+        state = (
+            jnp.concatenate([total, jnp.zeros((CHUNK, 2 * HEAD), F32)], axis=0),
+            jnp.concatenate([top, jnp.full((CHUNK, 1), NEG, F32)], axis=0),
+        )
+        total, top = lax.fori_loop(1, 3, lambda s, c: over(query, query_token, s, *c), state)
+        give_back(2, 0, total[0:CHUNK], top[0:CHUNK])
+        give_back(2, 1, total[CHUNK : 2 * CHUNK], top[CHUNK : 2 * CHUNK])
 
     def combine(k):
         total, low, top = own_o[k][:, 0:HEAD], own_o[k][:, HEAD : 2 * HEAD], own_m[k]
@@ -419,26 +441,23 @@
     a_last(1)
     finish_queries(0)
     a_last(2)
-    send_o_weight()
     project(1)
-    neighbours_arrive()
     finish_queries(1)
-    attend_own(0)
     project(2)
     finish_queries(2)
-    attend_other(0)
-    attend_own(1)
-    attend_other(1)
-    attend_own(2)
+    send_o_weight()
+    neighbours_arrive()
+    attend_own()
+    attend_early()
+    attend_last()
     combine(0)
-    attend_other(2)
+    combine(1)
     o_weight_arrive()
     stage_one(0)
-    combine(1)
+    combine(2)
     stage_one(1)
-    combine(2)
+    stage_one(2)
     finish(0)
-    stage_one(2)
     finish(1)
     finish(2)
 

time: 77.7 us -> 73.3 us (0.943)
  Pallas kernels: 75.3 us -> 70.9 us
    pallas_call x1, Pallas kernels: 75.3 us -> 70.9 us  [local(): pl.pallas_call(kernel, out_shape=jax.ShapeDtypeStruct((GROUP, 256), BF16)...]
where the time goes in v5:
time: 73.3 us; the launch traced here: 73.2 us
  Pallas kernels  70.9 us (97%)
  local copies, waits for them, and re-layouts  1.62 us (2%)
    pallas_call x1, Pallas kernels, local(): pl.pallas_call(kernel, out_shape=jax.ShapeDtypeStruct((GROUP, 256), BF16)...  70.9 us
    unnamed x1, local copies, waits for them, and re-layouts  1.62 us

profile of v5, /device:TPU:1, one launch (start us, length us, event | category | flops | bytes accessed | tf_op | source)
XLA Modules:
  0.0 73.2 jit_solution(2684022379275370640)
XLA Ops:
  0.7 70.9 %attention_sublayer.1 = bf16[384,256]{1,0:T(8,128)(2,1)} custom-call(bf16[48,8192]{1,0:T(8,128)(2,1)} %hidden_ref.1, bf16[8192]{0:T(1024)(128)(2,1)} %gain_ref.1, bf16[8192,128]{1,0:T(8,128)(2,1)} %qw_ref.1, bf16[128]{0:T(256)(128)(2,1)} %qb_ref.1, bf16[8192,128]{1,0:T(8,128)(2,1)} %kw_ref.1, bf16[128]{0:T(256)(128)(2,1)} %kb_ref.1, ...), custom_call_target="tpu_custom_call" | custom-call | tf_op jit(solution)/shard_map/attention_sublayer/pallas_call | solution.py:524
  71.6 1.6 %copy.18 = bf16[384,256]{1,0:T(8,128)(2,1)} copy(bf16[384,256]{1,0:T(8,128)(2,1)} %attention_sublayer.1) | data formatting | bytes 393216

commit v6 on v5

--- a/solution.py
+++ b/solution.py
@@ -39,10 +39,10 @@
 
 
 def kernel(
-    hidden_ref, gain_ref, qw_ref, qb_ref, kw_ref, kb_ref, vw_ref, vb_ref, ow_ref, ck_ref, cv_ref,
+    hidden_hbm, gain_ref, qw_ref, qb_ref, kw_ref, kb_ref, vw_ref, vb_ref, ow_ref, ck_ref, cv_ref,
     blocks_ref, counts_ref, start_ref, freq_ref,
     out_ref,
-    normed, gathered, q_mat, kv_mat, o_mat, cache_k, cache_v,
+    hidden_ref, normed, gathered, q_mat, kv_mat, o_mat, cache_k, cache_v,
     pre_k, pre_v, span_k, span_v, mask, cos_ref, sin_ref,
     halves, halves_in, queries, part_o, part_s, part_o_in, part_s_in,
     own_o, own_m, own_head, attended, one_out, one_in, mid,
@@ -74,49 +74,6 @@
             src_ref=src, dst_ref=dst, send_sem=send, recv_sem=recv, device_id=to, device_id_type=MESH
         )
 
-    sent = []
-
-    def send(src, dst, send_sem, recv_sem, to):
-        copy = remote(src, dst, send_sem, recv_sem, to)
-        copy.start()
-        sent.append(copy)
-
-    def arrive(dst, recv_sem):
-        remote(dst, dst, recv_sem, recv_sem, partner).wait_recv()
-
-    def load(src, dst, i):
-        copy = pltpu.make_async_copy(src, dst, local_sems.at[i])
-        copy.start()
-        return copy
-
-    load_k = load(ck_ref, cache_k, 0)
-    load_v = load(cv_ref, cache_v, 1)
-    load_kw = load(kw_ref, kv_mat.at[:, 0:HEAD], 2)
-    load_vw = load(vw_ref, kv_mat.at[:, HEAD : 2 * HEAD], 3)
-    own_cols = pl.ds(pl.multiple_of(core * HEAD, HEAD), HEAD)
-    load_qw = load(qw_ref.at[pl.ds(pl.multiple_of(core * HALF, HALF), HALF), :], q_mat.at[:, own_cols], 4)
-
-    def gather_place(cc):
-        return y * (1 - cc) + x * cc
-
-    def columns(cc, summed, place):
-        xx = summed * (1 - cc) + place * cc
-        yy = place * (1 - cc) + summed * cc
-        return pl.ds(pl.multiple_of((2 * (xx // 2) + cc) * 2048 + (4 * lax.rem(xx, 2) + yy) * 256, 256), 256)
-
-    def head_slot(cc):
-        return 2 * gather_place(cc) + core
-
-    def slot_of(index):
-        return pl.ds(pl.multiple_of(index * HEAD, HEAD), HEAD)
-
-    for q in range(4):
-        pltpu.make_async_copy(
-            ow_ref.at[:, columns(core, q, gather_place(core))],
-            o_mat.at[slot_of(head_slot(core)), pl.ds(q * 256, 256)],
-            local_sems.at[5],
-        ).start()
-
     barrier = pltpu.get_barrier_semaphore()
     partners = [partner]
     partners += [device(0, s, 0, c) for s in range(1, 4) for c in range(2)]
@@ -126,6 +83,50 @@
     partners += [device(dz, 0, 0) for dz in (1, -1, 3, -3)]
     for to in partners:
         pl.semaphore_signal(barrier, inc=1, device_id=to, device_id_type=MESH)
+
+    sent = []
+
+    def send(src, dst, send_sem, recv_sem, to):
+        copy = remote(src, dst, send_sem, recv_sem, to)
+        copy.start()
+        sent.append(copy)
+
+    def arrive(dst, recv_sem):
+        remote(dst, dst, recv_sem, recv_sem, partner).wait_recv()
+
+    def load(src, dst, i):
+        copy = pltpu.make_async_copy(src, dst, local_sems.at[i])
+        copy.start()
+        return copy
+
+    load_hidden = load(hidden_hbm, hidden_ref, 6)
+    load_k = load(ck_ref, cache_k, 0)
+    load_v = load(cv_ref, cache_v, 1)
+    load_kw = load(kw_ref, kv_mat.at[:, 0:HEAD], 2)
+    load_vw = load(vw_ref, kv_mat.at[:, HEAD : 2 * HEAD], 3)
+    own_cols = pl.ds(pl.multiple_of(core * HEAD, HEAD), HEAD)
+    load_qw = load(qw_ref.at[pl.ds(pl.multiple_of(core * HALF, HALF), HALF), :], q_mat.at[:, own_cols], 4)
+
+    def gather_place(cc):
+        return y * (1 - cc) + x * cc
+
+    def columns(cc, summed, place):
+        xx = summed * (1 - cc) + place * cc
+        yy = place * (1 - cc) + summed * cc
+        return pl.ds(pl.multiple_of((2 * (xx // 2) + cc) * 2048 + (4 * lax.rem(xx, 2) + yy) * 256, 256), 256)
+
+    def head_slot(cc):
+        return 2 * gather_place(cc) + core
+
+    def slot_of(index):
+        return pl.ds(pl.multiple_of(index * HEAD, HEAD), HEAD)
+
+    for q in range(4):
+        pltpu.make_async_copy(
+            ow_ref.at[:, columns(core, q, gather_place(core))],
+            o_mat.at[slot_of(head_slot(core)), pl.ds(q * 256, 256)],
+            local_sems.at[5],
+        ).start()
 
     def rows_of(shard):
         return pl.ds(pl.multiple_of(shard * PIECE, PIECE), PIECE)
@@ -189,6 +190,7 @@
         a_arrive(k, 1, far)
         forward(k, 1, far, x_down)
 
+    load_hidden.wait()
     normalise(0)
     normalise(1)
     normalise(2)
@@ -447,14 +449,14 @@
     finish_queries(2)
     send_o_weight()
     neighbours_arrive()
-    attend_own()
     attend_early()
     attend_last()
+    attend_own()
     combine(0)
     combine(1)
+    combine(2)
     o_weight_arrive()
     stage_one(0)
-    combine(2)
     stage_one(1)
     stage_one(2)
     finish(0)
@@ -481,6 +483,7 @@
     hbm = pl.BlockSpec(memory_space=pl.ANY)
     dma = pltpu.SemaphoreType.DMA
     scratch = [
+        pltpu.VMEM((SHARD, WIDTH), BF16),
         pltpu.VMEM((SHARD, WIDTH), BF16),
         pltpu.VMEM((CHUNKS, 2, CHUNK, QUART), BF16),
         pltpu.VMEM((HALF, 2 * HEAD), BF16),
@@ -509,7 +512,7 @@
         pltpu.VMEM((CHUNKS, 3, CHUNK, 256), BF16),
         pltpu.VMEM((CHUNKS, 3, CHUNK, 256), BF16),
         pltpu.VMEM((CHUNKS, CHUNK, 256), F32),
-        dma((6,)),
+        dma((7,)),
         dma((CHUNKS, 14)), dma((CHUNKS, 2, SHARDS)),
         dma((8,)), dma((1,)), dma((8,)),
         dma((2, 2)), dma((2, 3)),
@@ -524,7 +527,7 @@
     return pl.pallas_call(
         kernel,
         out_shape=jax.ShapeDtypeStruct((GROUP, 256), BF16),
-        in_specs=[vmem, vmem, hbm, vmem, hbm, vmem, hbm, vmem, hbm, hbm, hbm, smem, smem, smem, vmem],
+        in_specs=[hbm, vmem, hbm, vmem, hbm, vmem, hbm, vmem, hbm, hbm, hbm, smem, smem, smem, vmem],
         out_specs=vmem,
         scratch_shapes=scratch,
         compiler_params=pltpu.CompilerParams(

time: 73.3 us -> 68.2 us (0.930)
  Pallas kernels: 70.9 us -> 65.7 us
    pallas_call x1, Pallas kernels: 70.9 us -> 65.7 us  [local(): pl.pallas_call(kernel, out_shape=jax.ShapeDtypeStruct((GROUP, 256), BF16)...]
where the time goes in v6:
time: 68.2 us; the launch traced here: 68 us
  Pallas kernels  65.7 us (96%)
  local copies, waits for them, and re-layouts  1.62 us (2%)
    pallas_call x1, Pallas kernels, local(): pl.pallas_call(kernel, out_shape=jax.ShapeDtypeStruct((GROUP, 256), BF16)...  65.7 us
    unnamed x1, local copies, waits for them, and re-layouts  1.62 us

profile of v6, /device:TPU:1, one launch (start us, length us, event | category | flops | bytes accessed | tf_op | source)
XLA Modules:
  0.0 68.0 jit_solution(5219809919336618430)
XLA Ops:
  0.7 65.7 %attention_sublayer.1 = bf16[384,256]{1,0:T(8,128)(2,1)} custom-call(bf16[48,8192]{1,0:T(8,128)(2,1)} %hidden_hbm.1, bf16[8192]{0:T(1024)(128)(2,1)} %gain_ref.1, bf16[8192,128]{1,0:T(8,128)(2,1)} %qw_ref.1, bf16[128]{0:T(256)(128)(2,1)} %qb_ref.1, bf16[8192,128]{1,0:T(8,128)(2,1)} %kw_ref.1, bf16[128]{0:T(256)(128)(2,1)} %kb_ref.1, ...), custom_call_target="tpu_custom_call" | custom-call | tf_op jit(solution)/shard_map/attention_sublayer/pallas_call | solution.py:527
  66.4 1.6 %copy.18 = bf16[384,256]{1,0:T(8,128)(2,1)} copy(bf16[384,256]{1,0:T(8,128)(2,1)} %attention_sublayer.1) | data formatting | bytes 393216

commit v7 on v6

--- a/solution.py
+++ b/solution.py
@@ -335,30 +335,27 @@
         send(part_o.at[k, i], part_o_in.at[k, i], p_send.at[k, i, 0], p_recv.at[k, i, 0], back)
         send(part_s.at[k, i], part_s_in.at[k, i], p_send.at[k, i, 1], p_recv.at[k, i, 1], back)
 
-    def attend_early():
-        for i, (source, first) in enumerate(((1, 0), (2, 1))):
-            for k in range(2):
-                arrive(queries.at[source, k], q_recv.at[k, i])
-            query = queries[source, 0:2].reshape(2 * CHUNK, HEAD)
-            total, top = attend(query, tokens_of(source, range(2)), first)
-            for k in range(2):
-                rows = slice(k * CHUNK, (k + 1) * CHUNK)
-                give_back(k, i, total[rows], top[rows])
-
-    def attend_last():
-        arrive(queries.at[1, 2], q_recv.at[2, 0])
-        arrive(queries.at[2, 2], q_recv.at[2, 1])
-        below, above = tokens_of(1, (2,)), tokens_of(2, (2,))
-        total, top = over(queries[1, 2], below, 0, None, None)
-        query = jnp.concatenate([queries[1, 2], queries[2, 2]], axis=0)
+    def attend_sources(begin, end):
+        chunks = range(begin, end)
+        rows = (end - begin) * CHUNK
+        for i in range(2):
+            for k in chunks:
+                arrive(queries.at[1 + i, k], q_recv.at[k, i])
+        below, above = tokens_of(1, chunks), tokens_of(2, chunks)
+        lower = queries[1, begin:end].reshape(rows, HEAD)
+        upper = queries[2, begin:end].reshape(rows, HEAD)
+        total, top = over(lower, below, 0, None, None)
+        query = jnp.concatenate([lower, upper], axis=0)
         query_token = jnp.concatenate([below, above], axis=0)
         state = (
-            jnp.concatenate([total, jnp.zeros((CHUNK, 2 * HEAD), F32)], axis=0),
-            jnp.concatenate([top, jnp.full((CHUNK, 1), NEG, F32)], axis=0),
+            jnp.concatenate([total, jnp.zeros((rows, 2 * HEAD), F32)], axis=0),
+            jnp.concatenate([top, jnp.full((rows, 1), NEG, F32)], axis=0),
         )
         total, top = lax.fori_loop(1, 3, lambda s, c: over(query, query_token, s, *c), state)
-        give_back(2, 0, total[0:CHUNK], top[0:CHUNK])
-        give_back(2, 1, total[CHUNK : 2 * CHUNK], top[CHUNK : 2 * CHUNK])
+        for i in range(2):
+            for k in chunks:
+                at = i * rows + (k - begin) * CHUNK
+                give_back(k, i, total[at : at + CHUNK], top[at : at + CHUNK])
 
     def combine(k):
         total, low, top = own_o[k][:, 0:HEAD], own_o[k][:, HEAD : 2 * HEAD], own_m[k]
@@ -449,8 +446,8 @@
     finish_queries(2)
     send_o_weight()
     neighbours_arrive()
-    attend_early()
-    attend_last()
+    attend_sources(0, 2)
+    attend_sources(2, 3)
     attend_own()
     combine(0)
     combine(1)

time: 68.2 us -> 69 us (1.012)
  Pallas kernels: 65.7 us -> 66.6 us
    pallas_call x1, Pallas kernels: 65.7 us -> 66.6 us  [local(): pl.pallas_call(kernel, out_shape=jax.ShapeDtypeStruct((GROUP, 256), BF16)...]
where the time goes in v7:
time: 69 us; the launch traced here: 68.8 us
  Pallas kernels  66.6 us (97%)
  local copies, waits for them, and re-layouts  1.62 us (2%)
    pallas_call x1, Pallas kernels, local(): pl.pallas_call(kernel, out_shape=jax.ShapeDtypeStruct((GROUP, 256), BF16)...  66.6 us
    unnamed x1, local copies, waits for them, and re-layouts  1.62 us

profile of v7, /device:TPU:1, one launch (start us, length us, event | category | flops | bytes accessed | tf_op | source)
XLA Modules:
  0.0 68.8 jit_solution(1444057529065014147)
XLA Ops:
  0.7 66.6 %attention_sublayer.1 = bf16[384,256]{1,0:T(8,128)(2,1)} custom-call(bf16[48,8192]{1,0:T(8,128)(2,1)} %hidden_hbm.1, bf16[8192]{0:T(1024)(128)(2,1)} %gain_ref.1, bf16[8192,128]{1,0:T(8,128)(2,1)} %qw_ref.1, bf16[128]{0:T(256)(128)(2,1)} %qb_ref.1, bf16[8192,128]{1,0:T(8,128)(2,1)} %kw_ref.1, bf16[128]{0:T(256)(128)(2,1)} %kb_ref.1, ...), custom_call_target="tpu_custom_call" | custom-call | tf_op jit(solution)/shard_map/attention_sublayer/pallas_call | solution.py:524
  67.2 1.6 %copy.18 = bf16[384,256]{1,0:T(8,128)(2,1)} copy(bf16[384,256]{1,0:T(8,128)(2,1)} %attention_sublayer.1) | data formatting | bytes 393216
